TPU v7x, 32 devices: a whole 2x2x4 slice. The times are simulated.
32 devices in a mesh: shots: 2 (over x), depth: 16 (over z, y, core).
Axes of the slice: x: 2, y: 2, z: 4, core: 2. Of those that a mesh axis runs over, the one named last changes fastest.
Arguments:
- fields_in: float32 [16, 4, 64, 2048], P('depth', None, 'shots'), parts along dimension 2, may hold values from -6 to 6
- flight_angular: float32 [16, 64], P('depth', 'shots'), parts along dimension 1, may hold values from 0.6 to 3
- wavelet: float32 [3, 2, 64], P(None, None, 'shots'), parts along dimension 2, may hold values from -6 to 6
- surface_angular: float32 [3, 64], P(None, 'shots'), parts along dimension 1, may hold values from 0.6 to 3
- records: float32 [3, 2, 64, 1024], P(None, None, 'shots'), parts along dimension 2, may hold values from -6 to 6
- source_pos: int32 [2], P('shots'), parts along dimension 0, may hold values from 0 to 2047
- receiver_pos: int32 [2048], P('shots'), parts along dimension 0, may hold values from 0 to 2047
- vel_table: float32 [64, 16], P('depth'), may hold values from 1.5 to 4.5
- vel_index: int32 [64, 2048], P('depth'), may hold values from 0 to 15
Outputs:
- section: float32 [64, 4096], P('depth', 'shots'), parts along dimension 1
- fields_out: float32 [16, 4, 64, 2048], P('depth', None, 'shots'), parts along dimension 2
There are 2 independent parts, one for each index of `shots`. A program takes and returns all parts, laid end to end along the dimension named above; an argument that names none is the same for every part. Nothing has to cross between parts.
All inputs are finite; a program needn't handle non-finite values.
Results may differ from a plain program's by a relative error of at most 0.0003.
Values sent between devices are 32-bit elements; how exact they have to be, the bound alone decides.
No kernel may reach another device: no remote copies, remote signals or barrier semaphores. Data moves between devices by JAX's collectives and lax.ppermute only.
A program may use at most 64 MiB of HBM per device.

v0:
```python
import math

import jax
import jax.numpy as jnp
from jax import lax
from jax.experimental import pallas as pl
from jax.experimental.pallas import tpu as pltpu
from jax.sharding import PartitionSpec as P

TICKS = 3
SUB = 8
LANES = 128

depth_step = 1.0
lateral_scale = 0.03
damping = 0.3


def as_column(row):
    n = row.shape[1]
    shape = (n, n)
    same = lax.broadcasted_iota(jnp.int32, shape, 0) == lax.broadcasted_iota(jnp.int32, shape, 1)
    return jnp.sum(jnp.where(same, row, 0.0), axis=1, keepdims=True)


def three_pieces(value):
    high = value.astype(jnp.bfloat16)
    rest = value - high.astype(jnp.float32)
    mid = rest.astype(jnp.bfloat16)
    low = (rest - mid.astype(jnp.float32)).astype(jnp.bfloat16)
    return high, mid, low


def layer_tables(w_col, model, row, rows, width, levels):
    index = model[pl.ds(row, 1), :]
    speed = model[pl.ds(row + 4, 1), :][:, : 3 * levels]
    phase = w_col * (depth_step / speed)
    gain = (lateral_scale / 24.0) * speed / w_col
    table = jnp.concatenate([jnp.cos(phase), jnp.sin(phase), gain], axis=0)
    high, mid, low = three_pieces(table)
    lane = lax.broadcasted_iota(jnp.int32, table.shape, 1)
    pieces = jnp.where(
        lane < levels,
        high.astype(jnp.float32),
        jnp.where(lane < 2 * levels, mid.astype(jnp.float32), low.astype(jnp.float32)),
    ).astype(jnp.bfloat16)
    level = lax.broadcasted_iota(jnp.int32, (3 * levels, width), 0) % levels
    hot = jnp.where(level == index.astype(jnp.int32), 1.0, 0.0).astype(jnp.bfloat16)
    return jnp.dot(pieces, hot, preferred_element_type=jnp.float32)


def layer_tile(state, tables, r0, rows, emit):
    width = state.shape[2]
    blocks = width // LANES
    lane = lax.broadcasted_iota(jnp.int32, (SUB, LANES), 1)
    first, first2 = lane == 0, lane < 2
    last, last2 = lane == LANES - 1, lane >= LANES - 2
    zero = jnp.zeros((SUB, LANES), jnp.float32)
    cell, p1, p2, m1, m2, gains = {}, {}, {}, {}, {}, {}
    for j in (-1, blocks):
        p1[j] = p2[j] = m1[j] = m2[j] = [zero] * 4
    for j in range(blocks + 1):
        if j < blocks:
            at = pl.ds(j * LANES, LANES)
            sr, si, rr, ri = (state[c, pl.ds(r0, SUB), at] for c in range(4))
            cosine = tables[pl.ds(r0, SUB), at]
            sine = tables[pl.ds(rows + r0, SUB), at]
            gains[j] = tables[pl.ds(2 * rows + r0, SUB), at]
            cell[j] = [
                sr * cosine - si * sine,
                sr * sine + si * cosine,
                rr * cosine + ri * sine,
                ri * cosine - rr * sine,
            ]
            p1[j] = [pltpu.roll(v, 1, 1) for v in cell[j]]
            p2[j] = [pltpu.roll(v, 2, 1) for v in cell[j]]
            m1[j] = [pltpu.roll(v, LANES - 1, 1) for v in cell[j]]
            m2[j] = [pltpu.roll(v, LANES - 2, 1) for v in cell[j]]
        if j >= 1:
            k = j - 1
            spread = []
            for c in range(4):
                near = jnp.where(first, p1[k - 1][c], p1[k][c]) + jnp.where(last, m1[k + 1][c], m1[k][c])
                far = jnp.where(first2, p2[k - 1][c], p2[k][c]) + jnp.where(last2, m2[k + 1][c], m2[k][c])
                spread.append(16.0 * near - far - 30.0 * cell[k][c])
            g = gains[k]
            new = [
                cell[k][0] + g * (damping * spread[0] - spread[1]),
                cell[k][1] + g * (damping * spread[1] + spread[0]),
                cell[k][2] + g * (damping * spread[2] + spread[3]),
                cell[k][3] + g * (damping * spread[3] - spread[2]),
            ]
            at = pl.ds(k * LANES, LANES)
            for c in range(4):
                state[c, pl.ds(r0, SUB), at] = new[c]
            if emit is not None:
                emit(k, new[0] * new[2] + new[1] * new[3])


def surface_rows(t, f0, rows, wavelet, records, source_pos, receiver_pos, state, hits):
    width = state.shape[2]
    receivers = records.shape[3]
    hits[...] = jnp.where(
        lax.broadcasted_iota(jnp.int32, (width, receivers), 0) == receiver_pos[...], 1.0, 0.0
    ).astype(jnp.bfloat16)
    cells = lax.broadcasted_iota(jnp.int32, (rows, width), 1)
    spot = cells == source_pos[0]
    for c in range(2):
        strength = as_column(wavelet[t, pl.ds(c, 1), :])[f0 : f0 + rows]
        state[c] = jnp.where(spot, strength, 0.0)
        pieces = jnp.concatenate(three_pieces(records[t, c, f0 : f0 + rows, :]), axis=0)
        for x in range(0, width, 512):
            found = lax.dot_general(
                pieces,
                hits[x : x + 512, :],
                (((1,), (1,)), ((), ())),
                preferred_element_type=jnp.float32,
            )
            state[2 + c, :, x : x + 512] = found[:rows] + found[rows : 2 * rows] + found[2 * rows :]


def main_kernel(
    chunk, rows, devices, last_chunk,
    fields, angular, surface_angular, wavelet, records, source_pos, receiver_pos,
    model0, model1, model2, *rest,
):
    if last_chunk:
        earlier, sent, own, next1, next2, above, state, tables, totals, models, hits = rest
    else:
        sent, partial, state, tables, totals, models, hits = rest
    width = state.shape[2]
    f0 = chunk * rows
    d = lax.axis_index("depth")
    levels = 16
    for t, model in enumerate((model0, model1, model2)):
        models[8 * t : 8 * t + 8, :] = model[...]
    for c in range(4):
        state[c] = fields[0, c]
    w_own = as_column(angular[...])[f0 : f0 + rows]
    w_top = as_column(surface_angular[pl.ds(0, 1), :])[f0 : f0 + rows]

    def step(l, carry):
        @pl.when(jnp.logical_and(l == 4, d == devices - 1))
        def _():
            surface_rows(0, f0, rows, wavelet, records, source_pos, receiver_pos, state, hits)

        swapped = jnp.logical_and(l >= 4, d == devices - 1)
        w_col = jnp.where(swapped, w_top, w_own)
        row = 8 * (l // 4) + l % 4
        tables[...] = layer_tables(w_col, models, row, rows, width, levels)
        for r0 in range(0, rows, SUB):
            def emit(k, value):
                at = pl.ds(k * LANES, LANES)
                if r0 == 0:
                    totals[l, :, at] = value
                else:
                    totals[l, :, at] += value
            layer_tile(state, tables, r0, rows, emit)
        return carry

    lax.fori_loop(0, 4 * TICKS, step, 0)
    for c in range(4):
        sent[c * rows : (c + 1) * rows, :] = state[c]
    found = [jnp.sum(totals[l], axis=0, keepdims=True) for l in range(4 * TICKS)]
    if not last_chunk:
        for l in range(4 * TICKS):
            partial[l : l + 1, :] = found[l]
        return
    scale = 1.0 / math.sqrt(angular.shape[1])
    image = []
    for l in range(4 * TICKS):
        value = (found[l] + earlier[l : l + 1, :]) * scale
        if l >= 8:
            value = jnp.where(d == devices - 2, 0.0, value)
        image.append(value)
    apart = d == devices - 1

    def filtered(l):
        total = 0.0
        if 0 <= l < 4 * TICKS:
            total = 2.0 * image[l]
        if 0 <= l - 1:
            before = image[l - 1]
            total = total - 0.5 * (jnp.where(apart, 0.0, before) if l == 4 else before)
        if l + 1 < 4 * TICKS:
            after = image[l + 1]
            total = total - 0.5 * (jnp.where(apart, 0.0, after) if l == 3 else after)
        return total

    above[...] = filtered(-1)
    for l in range(4):
        own[l : l + 1, :] = filtered(l)
        next1[l : l + 1, :] = filtered(l + 4)
        next2[l : l + 1, :] = filtered(l + 8)
    sent[4 * rows : 4 * rows + 1, :] = filtered(12)


def top_kernel(
    above, surface_angular, wavelet, records, source_pos, receiver_pos, model,
    sent, extra, out, state, tables, totals, hits,
):
    width = state.shape[2]
    rows = state.shape[1]
    d = lax.axis_index("depth")
    sent[...] = jnp.zeros(sent.shape, jnp.float32)
    sent[3:4, :] = above[...]
    extra[...] = jnp.zeros(extra.shape, jnp.float32)

    @pl.when(d == 0)
    def _():
        surface_rows(2, 0, rows, wavelet, records, source_pos, receiver_pos, state, hits)

    @pl.when(d == 1)
    def _():
        surface_rows(1, 0, rows, wavelet, records, source_pos, receiver_pos, state, hits)
        w_col = as_column(surface_angular[pl.ds(1, 1), :])

        def step(l, carry):
            tables[...] = layer_tables(w_col, model, l, rows, width, 16)
            for r0 in range(0, rows, SUB):
                def emit(k, value):
                    at = pl.ds(k * LANES, LANES)
                    if r0 == 0:
                        totals[l, :, at] = value
                    else:
                        totals[l, :, at] += value
                layer_tile(state, tables, r0, rows, emit)
            return carry

        lax.fori_loop(0, 4, step, 0)
        scale = 1.0 / math.sqrt(rows)
        image = [jnp.sum(totals[l], axis=0, keepdims=True) * scale for l in range(4)]
        for l in range(4):
            total = 2.0 * image[l]
            if l > 0:
                total = total - 0.5 * image[l - 1]
            if l < 3:
                total = total - 0.5 * image[l + 1]
            sent[l : l + 1, :] = total + above[...] if l == 3 else total
        extra[...] = -0.5 * image[3]

    @pl.when(d < 2)
    def _():
        out[0] = state[...]


def close_kernel(
    first, relayed, second, top, own, from1, from2, below, extra, section, fields_out, sems,
):
    d = lax.axis_index("depth")
    rows = relayed.shape[0] // 4

    def move(source, base, start, count, slot):
        return [
            pltpu.make_async_copy(
                source.at[pl.ds(c * base, count), :],
                fields_out.at[0, c, pl.ds(start, count), :],
                sems.at[slot + c],
            )
            for c in range(4)
        ]

    def run(copies):
        for copy in copies:
            copy.start()

    local = d < 2
    is_relayed = jnp.logical_and(d % 4 == 1, d > 1)

    @pl.when(local)
    def _():
        run([pltpu.make_async_copy(top.at[0, c, pl.ds(0, rows), :], fields_out.at[0, c, pl.ds(0, rows), :], sems.at[c]) for c in range(4)])
        run([pltpu.make_async_copy(top.at[0, c, pl.ds(rows, rows), :], fields_out.at[0, c, pl.ds(rows, rows), :], sems.at[4 + c]) for c in range(4)])

    @pl.when(jnp.logical_not(local))
    def _():
        run(move(second, rows, rows, rows, 4))

        @pl.when(is_relayed)
        def _():
            run(move(relayed, rows, 0, rows, 0))

        @pl.when(jnp.logical_not(is_relayed))
        def _():
            run(move(first, rows, 0, rows, 0))

    section[...] = own[...] + from1[...] + from2[...] + below[...]
    section[0:1, :] += extra[...] + second[4 * rows : 4 * rows + 1, :]
    for copy in move(first, rows, 0, rows, 0) + move(second, rows, rows, rows, 4):
        copy.wait()


VMEM = pl.BlockSpec(memory_space=pltpu.VMEM)
SMEM = pl.BlockSpec(memory_space=pltpu.SMEM)
ANY = pl.BlockSpec(memory_space=pl.ANY)
PARAMS = pltpu.CompilerParams(vmem_limit_bytes=40 * 2**20)


def f32(*shape):
    return jax.ShapeDtypeStruct(shape, jnp.float32)


def on_device(
    devices,
    fields_in, flight_angular, wavelet, surface_angular, records, source_pos, receiver_pos, vel_table, vel_index,
):
    width = fields_in.shape[3]
    freqs = fields_in.shape[2]
    receivers = records.shape[3]
    levels = vel_table.shape[1]
    rows = freqs // 2
    axis = "depth"
    positions = receiver_pos.reshape(1, receivers)
    model = jnp.concatenate(
        [
            vel_index.astype(jnp.float32),
            jnp.pad(jnp.concatenate([vel_table] * 3, axis=1), ((0, 0), (0, width - 3 * levels))),
        ],
        axis=0,
    )
    last = devices - 1
    model1 = lax.ppermute(model, axis, [(i, (i - 1) % devices) for i in range(devices)])
    model2 = lax.ppermute(model, axis, [(i, i - 2) for i in range(2, devices)] + [(1, last)])
    model_above = lax.ppermute(model, axis, [(0, 1)])

    def main(chunk, earlier):
        last_chunk = earlier is not None
        ins = [fields_in, flight_angular, surface_angular, wavelet, records, source_pos, positions, model, model1, model2]
        specs = [
            pl.BlockSpec((1, 4, rows, width), lambda i: (0, 0, chunk, 0)),
            VMEM, VMEM, VMEM, VMEM, SMEM, VMEM, VMEM, VMEM, VMEM,
        ]
        if last_chunk:
            ins.append(earlier)
            specs.append(VMEM)
            outs = (f32(4 * rows + 8, width), f32(4, width), f32(4, width), f32(4, width), f32(1, width))
        else:
            outs = (f32(4 * rows, width), f32(4 * TICKS, width))

        def body(*refs):
            main_kernel(chunk, rows, devices, last_chunk, *refs)

        return pl.pallas_call(
            body,
            grid=(1,),
            out_shape=outs,
            in_specs=specs,
            out_specs=[VMEM] * len(outs),
            scratch_shapes=[
                pltpu.VMEM((4, rows, width), jnp.float32),
                pltpu.VMEM((3 * rows, width), jnp.float32),
                pltpu.VMEM((4 * TICKS, SUB, width), jnp.float32),
                pltpu.VMEM((24, width), jnp.float32),
                pltpu.VMEM((width, receivers), jnp.bfloat16),
            ],
            compiler_params=PARAMS,
            name="blocks",
        )(*ins)

    on = [(i, i + 3) for i in range(devices - 3)]
    direct = on + [(last, 2)]
    via = [(i, i - 1) if i % 4 == 2 else (i, j) for i, j in on] + [(last, 2)]
    relay = [(i, i + 4) for i in range(1, devices - 4, 4)]

    sent1, partial = main(0, None)
    first = lax.ppermute(sent1, axis, via)
    sent2, own, next1, next2, above = main(1, partial)
    second = lax.ppermute(sent2, axis, direct)
    relayed = lax.ppermute(first, axis, relay)
    from1 = lax.ppermute(next1, axis, [(i, (i + 1) % devices) for i in range(devices)])
    from2 = lax.ppermute(next2, axis, [(i, i + 2) for i in range(devices - 2)] + [(last, 1)])
    sent_up, extra, top = pl.pallas_call(
        top_kernel,
        out_shape=(f32(4, width), f32(1, width), f32(1, 4, freqs, width)),
        in_specs=[VMEM, VMEM, VMEM, VMEM, SMEM, VMEM, VMEM],
        out_specs=[VMEM] * 3,
        scratch_shapes=[
            pltpu.VMEM((4, freqs, width), jnp.float32),
            pltpu.VMEM((3 * freqs, width), jnp.float32),
            pltpu.VMEM((4, SUB, width), jnp.float32),
            pltpu.VMEM((width, receivers), jnp.bfloat16),
        ],
        compiler_params=PARAMS,
        name="top",
    )(above, surface_angular, wavelet, records, source_pos, positions, model_above)
    below = lax.ppermute(sent_up, axis, [(i, i - 1) for i in range(1, devices)])
    section, fields_out = pl.pallas_call(
        close_kernel,
        out_shape=(f32(4, width), f32(1, 4, freqs, width)),
        in_specs=[ANY, ANY, VMEM, ANY, VMEM, VMEM, VMEM, VMEM, VMEM],
        out_specs=[VMEM, ANY],
        scratch_shapes=[pltpu.SemaphoreType.DMA((8,))],
        compiler_params=PARAMS,
        name="close",
    )(first, relayed, second, top, own, from1, from2, below, extra)
    return section, fields_out


def solution(mesh):
    placed = (
        P("depth", None, "shots", None),
        P("depth", "shots"),
        P(None, None, "shots"),
        P(None, "shots"),
        P(None, None, "shots", None),
        P("shots"),
        P("shots"),
        P("depth", None),
        P("depth", None),
    )
    devices = mesh.shape["depth"]

    def run(*args):
        return on_device(devices, *args)

    return jax.shard_map(
        run,
        mesh=mesh,
        in_specs=placed,
        out_specs=(P("depth", "shots"), P("depth", None, "shots", None)),
        check_vma=False,
    )
```

profile of v0, /device:TPU:1, one launch (start us, length us, event | category | flops | bytes accessed | tf_op | source)
XLA Modules:
  0.0 63.1 jit_solution(9400265715193790985)
XLA Ops:
  0.6 0.0 copy-start.7
  0.6 0.9 %select_maximum_fusion = f32[4,2048]{1,0:T(4,128)S(1)} fusion(f32[4,16]{1,0:T(4,128)} %param.16), kind=kLoop, calls=%fused_computation.1 | loop fusion | flops 49152 | bytes 33024 | tf_op jit(solution)/shard_map/concatenate | solution.py:317
  1.5 0.0 copy-done.7
  1.5 0.0 copy-start.3
  1.5 0.0 copy-start.5
  1.6 0.0 copy-start.4
  1.6 7.0 %collective-permute-start.1 = (f32[8,2048]{1,0:T(8,128)S(1)}, f32[8,2048]{1,0:T(8,128)S(1)}, u32[]{:S(2)}, u32[]{:S(2)}) collective-permute-start(f32[8,2048]{1,0:T(8,128)S(1)} %pad_maximum_fusion.refs_7_), channel_id=1, source_target_pairs={{2,0},{3,1},{4,2},{5,3},{6,4},{7,5},{8,6},{9,7},{10,8},{11,9},{12,... | collective-permute-start | bytes 196616 | tf_op jit(solution)/shard_map/ppermute | solution.py:323
  8.6 0.1 collective-permute-start
  9.3 0.0 copy-start.6
  9.3 0.6 collective-permute-done.1.refs_9_
  9.9 2.4 %collective-permute-done.refs_8_ = f32[8,2048]{1,0:T(8,128)S(1)} collective-permute-done((f32[8,2048]{1,0:T(8,128)S(1)}, f32[8,2048]{1,0:T(8,128)S(1)}, u32[]{:S(2)}, u32[]{:S(2)}) %collective-permute-start) | collective-permute-done | bytes 65568 | tf_op jit(solution)/shard_map/ppermute | solution.py:322
  12.4 0.0 copy-done.3
  12.4 0.0 copy-done.5
  12.4 0.0 copy-done.4
  12.4 0.0 copy-done.6
  12.4 0.0 copy-start
  12.4 1.1 %copy-done = f32[3,2,32,1024]{3,2,1,0:T(8,128)S(1)} copy-done((f32[3,2,32,1024]{3,2,1,0:T(8,128)S(1)}, f32[3,2,32,1024]{3,2,1,0:T(8,128)}, u32[]{:S(2)}) %copy-start) | copy-done | bytes 786456
  13.5 0.0 copy-start.2
  13.5 1.2 %copy-done.2 = f32[1,4,32,2048]{3,2,1,0:T(8,128)S(1)} copy-done((f32[1,4,32,2048]{3,2,1,0:T(8,128)S(1)}, f32[1,4,32,2048]{3,2,1,0:T(8,128)}, u32[]{:S(2)}) %copy-start.2) | copy-done | bytes 1048600
  14.7 10.4 %blocks.2 = (f32[64,2048]{1,0:T(8,128)S(1)}, f32[12,2048]{1,0:T(8,128)S(1)}) custom-call(f32[1,4,32,2048]{3,2,1,0:T(8,128)S(1)} %copy-done.2, f32[1,32]{1,0:T(1,128)S(1)} %copy-done.6, f32[3,32]{1,0:T(4,128)S(1)} %copy-done.5, f32[3,2,32]{2,1,0:T(2,128)S(1)} %copy-done.4, f32[3,2,32,1024]{3,2,1,0:T(8,128)S(1)} %copy-done, s32[1]{0:T(128)S(6)} %copy.11.refs_5_.source_pos, ...), custom_call_target="tpu_custom_call" | custom-call | tf_op jit(solution)/shard_map/blocks/pallas_call | solution.py:343
  25.1 1.9 %collective-permute-start.2 = (f32[64,2048]{1,0:T(8,128)S(1)}, f32[64,2048]{1,0:T(8,128)S(1)}, u32[]{:S(2)}, u32[]{:S(2)}) collective-permute-start(f32[64,2048]{1,0:T(8,128)S(1)} %get-tuple-element.12), channel_id=1, source_target_pairs={{0,3},{1,4},{2,1},{3,6},{4,7},{5,8},{6,5},{7,10},{8,11},{9,12},{10... | collective-permute-start | bytes 1572872 | tf_op jit(solution)/shard_map/ppermute | solution.py:366
  27.0 0.0 copy-start.1
  27.0 10.6 %blocks.3 = (f32[72,2048]{1,0:T(8,128)S(1)}, f32[4,2048]{1,0:T(4,128)S(1)}, f32[4,2048]{1,0:T(4,128)S(1)}, f32[4,2048]{1,0:T(4,128)S(1)}, f32[1,2048]{1,0:T(1,128)S(1)}) custom-call(f32[1,4,32,2048]{3,2,1,0:T(8,128)S(1)} %copy-done.2, f32[1,32]{1,0:T(1,128)S(1)} %copy-done.6, f32[3,32]{1,0:T(4,128)S(1)} %copy-done.5, f32[3,2,32]{2,1,0:T(2,128)S(1)} %copy-done.4, ...), custom_call_target="tpu_custom_call" | custom-call | tf_op jit(solution)/shard_map/blocks/pallas_call | solution.py:343
  37.7 2.6 %collective-permute-start.4 = (f32[72,2048]{1,0:T(8,128)S(1)}, f32[72,2048]{1,0:T(8,128)S(1)}, u32[]{:S(2)}, u32[]{:S(2)}) collective-permute-start(f32[72,2048]{1,0:T(8,128)S(1)} %get-tuple-element.14), channel_id=1, source_target_pairs={{0,3},{1,4},{2,5},{3,6},{4,7},{5,8},{6,9},{7,10},{8,11},{9,12},{10... | collective-permute-start | bytes 1769480 | tf_op jit(solution)/shard_map/ppermute | solution.py:368
  40.2 0.0 collective-permute-done.2.first
  40.2 3.2 %collective-permute-start.3 = (f32[64,2048]{1,0:T(8,128)S(1)}, f32[64,2048]{1,0:T(8,128)S(1)}, u32[]{:S(2)}, u32[]{:S(2)}) collective-permute-start(f32[64,2048]{1,0:T(8,128)S(1)} %collective-permute-done.2.first), channel_id=1, source_target_pairs={{1,5},{5,9},{9,13},{17,21},{21,25},{25,29}} | collective-permute-start | bytes 1572872 | tf_op jit(solution)/shard_map/ppermute | solution.py:369
  43.4 1.3 %collective-permute-start.5 = (f32[8,2048]{1,0:T(8,128)S(1)}, f32[8,2048]{1,0:T(8,128)S(1)}, u32[]{:S(2)}, u32[]{:S(2)}) collective-permute-start(f32[8,2048]{1,0:T(8,128)S(1)} %pad_maximum_fusion.refs_7_), channel_id=1, source_target_pairs={{0,1},{16,17}} | collective-permute-start | bytes 196616 | tf_op jit(solution)/shard_map/ppermute | solution.py:324
  44.7 0.1 collective-permute-start.6
  44.8 1.9 %collective-permute-start.7 = (f32[4,2048]{1,0:T(4,128)S(1)}, f32[4,2048]{1,0:T(4,128)S(1)}, u32[]{:S(2)}, u32[]{:S(2)}) collective-permute-start(f32[4,2048]{1,0:T(4,128)S(1)} %get-tuple-element.19), channel_id=1, source_target_pairs={{0,2},{1,3},{2,4},{3,5},{4,6},{5,7},{6,8},{7,9},{8,10},{9,11},{10,... | collective-permute-start | bytes 98312 | tf_op jit(solution)/shard_map/ppermute | solution.py:371
  46.7 0.0 collective-permute-done.5.model
  46.7 0.0 copy-done.1
  46.8 9.3 %top.1 = (f32[4,2048]{1,0:T(4,128)S(1)}, f32[1,2048]{1,0:T(1,128)S(1)}, f32[1,4,32,2048]{3,2,1,0:T(8,128)S(1)}) custom-call(f32[1,2048]{1,0:T(1,128)S(1)} %get-tuple-element.15.above, f32[3,32]{1,0:T(4,128)S(1)} %copy-done.5, f32[3,2,32]{2,1,0:T(2,128)S(1)} %copy-done.4, f32[3,2,32,1024]{3,2,1,0:T(8,128)S(1)} %copy-done.1, s32[1]{0:T(128)S(6)} %copy.11.refs_5_.source_pos, ...), custom_call_target="tpu_custom_call" | custom-call | tf_op jit(solution)/shard_map/top/pallas_call | solution.py:372
  56.1 1.9 %collective-permute-start.8 = (f32[4,2048]{1,0:T(4,128)S(1)}, f32[4,2048]{1,0:T(4,128)S(1)}, u32[]{:S(2)}, u32[]{:S(2)}) collective-permute-start(f32[4,2048]{1,0:T(4,128)S(1)} %get-tuple-element.20), channel_id=1, source_target_pairs={{1,0},{2,1},{3,2},{4,3},{5,4},{6,5},{7,6},{8,7},{9,8},{10,9},{11,1... | collective-permute-start | bytes 98312 | tf_op jit(solution)/shard_map/ppermute | solution.py:386
  58.0 0.0 collective-permute-done.6.from1
  58.0 0.0 collective-permute-done.7.from2
  58.0 3.3 %collective-permute-done.8.below = f32[4,2048]{1,0:T(4,128)S(1)} collective-permute-done((f32[4,2048]{1,0:T(4,128)S(1)}, f32[4,2048]{1,0:T(4,128)S(1)}, u32[]{:S(2)}, u32[]{:S(2)}) %collective-permute-start.8) | collective-permute-done | bytes 32800 | tf_op jit(solution)/shard_map/ppermute | solution.py:386
  61.3 0.0 collective-permute-done.4.second
  61.3 0.0 collective-permute-done.3.relayed
  61.3 1.6 %close.1 = (f32[4,2048]{1,0:T(4,128)}, f32[1,4,32,2048]{3,2,1,0:T(8,128)}) custom-call(f32[64,2048]{1,0:T(8,128)S(1)} %collective-permute-done.2.first, f32[64,2048]{1,0:T(8,128)S(1)} %collective-permute-done.3.relayed, f32[72,2048]{1,0:T(8,128)S(1)} %collective-permute-done.4.second, f32[1,4,32,2048]{3,2,1,0:T(8,128)S(1)} %get-tuple-element.16.top, ...), custom_call_target="tpu_custom_call" | custom-call | tf_op jit(solution)/shard_map/close/pallas_call | solution.py:387
  (2 shorter events, 0.0 us)
Async XLA Ops:
  0.6 0.9 %copy-start.7 = (s32[4,2048]{1,0:T(4,128)S(1)}, s32[4,2048]{1,0:T(4,128)}, u32[]{:S(2)}) copy-start(s32[4,2048]{1,0:T(4,128)} %param.17) | copy-start | bytes 98308
  1.5 10.8 %copy-start.3 = (s32[1024]{0:T(1024)S(1)}, s32[1024]{0:T(1024)}, u32[]{:S(2)}) copy-start(s32[1024]{0:T(1024)} %param.15) | copy-start | bytes 12292
  1.5 10.8 %copy-start.5 = (f32[3,32]{1,0:T(4,128)S(1)}, f32[3,32]{1,0:T(4,128)}, u32[]{:S(2)}) copy-start(f32[3,32]{1,0:T(4,128)} %surface_angular.1) | copy-start | bytes 1156
  1.6 10.8 %copy-start.4 = (f32[3,2,32]{2,1,0:T(2,128)S(1)}, f32[3,2,32]{2,1,0:T(2,128)}, u32[]{:S(2)}) copy-start(f32[3,2,32]{2,1,0:T(2,128)} %wavelet.1) | copy-start | bytes 2308
  1.6 8.3 %collective-permute-start.1 = (f32[8,2048]{1,0:T(8,128)S(1)}, f32[8,2048]{1,0:T(8,128)S(1)}, u32[]{:S(2)}, u32[]{:S(2)}) collective-permute-start(f32[8,2048]{1,0:T(8,128)S(1)} %pad_maximum_fusion.refs_7_), channel_id=1, source_target_pairs={{2,0},{3,1},{4,2},{5,3},{6,4},{7,5},{8,6},{9,7},{10,8},{11,9},{12,... | collective-permute-start | bytes 196616 | tf_op jit(solution)/shard_map/ppermute | solution.py:323
  8.6 3.7 %collective-permute-start = (f32[8,2048]{1,0:T(8,128)S(1)}, f32[8,2048]{1,0:T(8,128)S(1)}, u32[]{:S(2)}, u32[]{:S(2)}) collective-permute-start(f32[8,2048]{1,0:T(8,128)S(1)} %pad_maximum_fusion.refs_7_), channel_id=1, source_target_pairs={{0,15},{1,0},{2,1},{3,2},{4,3},{5,4},{6,5},{7,6},{8,7},{9,8},{10,9... | collective-permute-start | bytes 196616 | tf_op jit(solution)/shard_map/ppermute | solution.py:322
  9.3 3.0 %copy-start.6 = (f32[1,32]{1,0:T(1,128)S(1)}, f32[1,32]{1,0:T(1,128)}, u32[]{:S(2)}) copy-start(f32[1,32]{1,0:T(1,128)} %refs_1_.3) | copy-start | bytes 388
  12.4 1.1 %copy-start = (f32[3,2,32,1024]{3,2,1,0:T(8,128)S(1)}, f32[3,2,32,1024]{3,2,1,0:T(8,128)}, u32[]{:S(2)}) copy-start(f32[3,2,32,1024]{3,2,1,0:T(8,128)} %records.1) | copy-start | bytes 2359300
  13.5 1.2 %copy-start.2 = (f32[1,4,32,2048]{3,2,1,0:T(8,128)S(1)}, f32[1,4,32,2048]{3,2,1,0:T(8,128)}, u32[]{:S(2)}) copy-start(f32[1,4,32,2048]{3,2,1,0:T(8,128)} %refs_0_.3) | copy-start | bytes 3145732
  25.1 15.1 %collective-permute-start.2 = (f32[64,2048]{1,0:T(8,128)S(1)}, f32[64,2048]{1,0:T(8,128)S(1)}, u32[]{:S(2)}, u32[]{:S(2)}) collective-permute-start(f32[64,2048]{1,0:T(8,128)S(1)} %get-tuple-element.12), channel_id=1, source_target_pairs={{0,3},{1,4},{2,1},{3,6},{4,7},{5,8},{6,5},{7,10},{8,11},{9,12},{10... | collective-permute-start | bytes 1572872 | tf_op jit(solution)/shard_map/ppermute | solution.py:366
  27.0 19.7 %copy-start.1 = (f32[3,2,32,1024]{3,2,1,0:T(8,128)S(1)}, f32[3,2,32,1024]{3,2,1,0:T(8,128)}, u32[]{:S(2)}) copy-start(f32[3,2,32,1024]{3,2,1,0:T(8,128)} %records.1) | copy-start | bytes 2359300
  37.7 23.7 %collective-permute-start.4 = (f32[72,2048]{1,0:T(8,128)S(1)}, f32[72,2048]{1,0:T(8,128)S(1)}, u32[]{:S(2)}, u32[]{:S(2)}) collective-permute-start(f32[72,2048]{1,0:T(8,128)S(1)} %get-tuple-element.14), channel_id=1, source_target_pairs={{0,3},{1,4},{2,5},{3,6},{4,7},{5,8},{6,9},{7,10},{8,11},{9,12},{10... | collective-permute-start | bytes 1769480 | tf_op jit(solution)/shard_map/ppermute | solution.py:368
  40.2 21.1 %collective-permute-start.3 = (f32[64,2048]{1,0:T(8,128)S(1)}, f32[64,2048]{1,0:T(8,128)S(1)}, u32[]{:S(2)}, u32[]{:S(2)}) collective-permute-start(f32[64,2048]{1,0:T(8,128)S(1)} %collective-permute-done.2.first), channel_id=1, source_target_pairs={{1,5},{5,9},{9,13},{17,21},{21,25},{25,29}} | collective-permute-start | bytes 1572872 | tf_op jit(solution)/shard_map/ppermute | solution.py:369
  43.4 3.3 %collective-permute-start.5 = (f32[8,2048]{1,0:T(8,128)S(1)}, f32[8,2048]{1,0:T(8,128)S(1)}, u32[]{:S(2)}, u32[]{:S(2)}) collective-permute-start(f32[8,2048]{1,0:T(8,128)S(1)} %pad_maximum_fusion.refs_7_), channel_id=1, source_target_pairs={{0,1},{16,17}} | collective-permute-start | bytes 196616 | tf_op jit(solution)/shard_map/ppermute | solution.py:324
  44.7 13.3 %collective-permute-start.6 = (f32[4,2048]{1,0:T(4,128)S(1)}, f32[4,2048]{1,0:T(4,128)S(1)}, u32[]{:S(2)}, u32[]{:S(2)}) collective-permute-start(f32[4,2048]{1,0:T(4,128)S(1)} %get-tuple-element.18), channel_id=1, source_target_pairs={{0,1},{1,2},{2,3},{3,4},{4,5},{5,6},{6,7},{7,8},{8,9},{9,10},{10,1... | collective-permute-start | bytes 98312 | tf_op jit(solution)/shard_map/ppermute | solution.py:370
  44.8 13.2 %collective-permute-start.7 = (f32[4,2048]{1,0:T(4,128)S(1)}, f32[4,2048]{1,0:T(4,128)S(1)}, u32[]{:S(2)}, u32[]{:S(2)}) collective-permute-start(f32[4,2048]{1,0:T(4,128)S(1)} %get-tuple-element.19), channel_id=1, source_target_pairs={{0,2},{1,3},{2,4},{3,5},{4,6},{5,7},{6,8},{7,9},{8,10},{9,11},{10,... | collective-permute-start | bytes 98312 | tf_op jit(solution)/shard_map/ppermute | solution.py:371
  56.1 5.2 %collective-permute-start.8 = (f32[4,2048]{1,0:T(4,128)S(1)}, f32[4,2048]{1,0:T(4,128)S(1)}, u32[]{:S(2)}, u32[]{:S(2)}) collective-permute-start(f32[4,2048]{1,0:T(4,128)S(1)} %get-tuple-element.20), channel_id=1, source_target_pairs={{1,0},{2,1},{3,2},{4,3},{5,4},{6,5},{7,6},{8,7},{9,8},{10,9},{11,1... | collective-permute-start | bytes 98312 | tf_op jit(solution)/shard_map/ppermute | solution.py:386
where the time goes:
time: 63.6 us; the launch traced here: 63.1 us
  Pallas kernels  32 us (50%)
  starting transfers between devices  19.9 us (31%)
  waiting for transfers between devices  6.32 us (10%)
  local copies, waits for them, and re-layouts  2.39 us (4%)
  between operations  1.65 us (3%)
  other arithmetic  0.89 us (1%)
    pallas_call x2, Pallas kernels, main(): pl.pallas_call(body, grid=(1,), out_shape=outs, in_specs=specs, out_specs...  21 us
    pallas_call x1, Pallas kernels, on_device(): pl.pallas_call(top_kernel, out_shape=(f32(4, width), f32(1, width), f32(1...  9.33 us
    ppermute x1, starting transfers between devices, on_device(): lax.ppermute(model, axis, [(i, i - 2) for i in range(2, devices)] + [(1,...  7.02 us
    ppermute x1, waiting for transfers between devices, on_device(): below = lax.ppermute(sent_up, axis, [(i, i - 1) for i in range(1, devices)])  3.28 us
    ppermute x1, starting transfers between devices, on_device(): relayed = lax.ppermute(first, axis, relay)  3.2 us
    ppermute x1, starting transfers between devices, on_device(): second = lax.ppermute(sent2, axis, direct)  2.56 us
    ppermute x1, waiting for transfers between devices, on_device(): lax.ppermute(model, axis, [(i, (i - 1) % devices) for i in range(devices)])  2.43 us
    unnamed x16, local copies, waits for them, and re-layouts  2.39 us
  transfers between devices with their start and end apart: 9, of which 3 were waited for; matrix products, arithmetic and copies ran while one was open for 0% of the time, Pallas kernels for 32%

commit v1 on v0

v1 whole, which is shorter than its diff:
```python
import math

import jax
import jax.numpy as jnp
from jax import lax
from jax.experimental import pallas as pl
from jax.experimental.pallas import tpu as pltpu
from jax.sharding import PartitionSpec as P

TICKS = 3
SUB = 8
LANES = 128
LAYERS = 4

depth_step = 1.0
lateral_scale = 0.03
damping = 0.3


COS = (0.9999999956, -0.4999999227, 0.04166644492, -0.001388656022, 2.469073179e-05, -2.510758575e-07)
SINC = (0.9999999997, -0.1666666607, 0.00833331612, -0.0001983946321, 2.747139839e-06, -2.315705927e-08)


def horner(coefficients, z):
    total = jnp.full(z.shape, coefficients[-1], jnp.float32)
    for c in coefficients[-2::-1]:
        total = total * z + c
    return total


def iota(shape, axis):
    return lax.broadcasted_iota(jnp.int32, shape, axis)


def as_column(row):
    n = row.shape[1]
    return jnp.sum(jnp.where(iota((n, n), 0) == iota((n, n), 1), row, 0.0), axis=1, keepdims=True)


def repeated(column):
    n = column.shape[0]
    return jnp.sum(jnp.where(iota((n, LANES), 0) == iota((n, LANES), 1) % n, column, 0.0), axis=0, keepdims=True)


def pieces_of(value, count):
    found = []
    for i in range(count):
        piece = value.astype(jnp.bfloat16)
        found.append(piece)
        if i + 1 < count:
            value = value - piece.astype(jnp.float32)
    return found


class Shape:
    def __init__(self, rows, width):
        self.rows, self.width = rows, width
        self.parts = LANES // rows
        self.cells = width // self.parts
        self.steps = self.cells // SUB


def load_field(shape, natural, c, flat, state):
    for b in range(shape.cells // LANES):
        stacked = jnp.concatenate(
            [natural(q * shape.cells + b * LANES) for q in range(shape.parts)], axis=0
        )
        flat[b * LANES : (b + 1) * LANES, :] = stacked.T
    for k in range(shape.steps):
        state[c, k * SUB : (k + 1) * SUB, :] = flat[pl.ds(k, SUB, stride=shape.steps), :]


def turned_back(shape, ref, b):
    rows = []
    for x in range(b * LANES, (b + 1) * LANES, SUB):
        sub, k = x // shape.steps, x % shape.steps
        rows.append(ref[pl.ds(k * SUB + sub, SUB, stride=SUB), :])
    return jnp.concatenate(rows, axis=0).T


def store_field(shape, c, state, put):
    for b in range(shape.cells // LANES):
        turned = turned_back(shape, state.at[c], b)
        for q in range(shape.parts):
            put(q * shape.cells + b * LANES, turned[q * shape.rows : (q + 1) * shape.rows, :])


def load_slowness(shape, models, flat, slowness):
    count = LAYERS * shape.parts
    for b in range(shape.cells // LANES):
        rows = [m[:, b * LANES : (b + 1) * LANES] for m in models]
        rows.append(jnp.zeros((LANES - len(models) * count, LANES), jnp.float32))
        flat[b * LANES : (b + 1) * LANES, :] = jnp.concatenate(rows, axis=0).T
    for k in range(0, shape.steps, 2):
        pair = jnp.concatenate([flat[pl.ds(k + i, SUB, stride=shape.steps), :] for i in range(2)], axis=0)
        for i, piece in enumerate(pieces_of(pair, 3)):
            slowness[k * SUB : (k + 2) * SUB, i * LANES : (i + 1) * LANES] = piece


def layer_slowness(shape, l, slowness, spread):
    chosen = jnp.where(
        iota((LANES, LANES), 0) == l * shape.parts + iota((LANES, LANES), 1) // shape.rows, 1.0, 0.0
    ).astype(jnp.bfloat16)
    spread[...] = jnp.dot(slowness[...], jnp.concatenate([chosen] * 3, axis=0), preferred_element_type=jnp.float32)


def layer_step(shape, state, w_row, spread, products):
    n = shape.steps
    sub, lane = iota((SUB, LANES), 0), iota((SUB, LANES), 1)
    rows = shape.rows
    cell, gains = {}, {}
    gain = lateral_scale * depth_step / 24.0

    def below(v):
        r = pltpu.roll(v, 1, 0)
        return jnp.where(sub == 0, jnp.where(lane < rows, 0.0, pltpu.roll(r, rows, 1)), r)

    def above(v):
        r = pltpu.roll(v, SUB - 1, 0)
        return jnp.where(sub == SUB - 1, jnp.where(lane >= LANES - rows, 0.0, pltpu.roll(r, LANES - rows, 1)), r)

    def turn(k):
        at = pl.ds(k * SUB, SUB)
        sr, si, rr, ri = (state[c, at, :] for c in range(4))
        phase = w_row * spread[at, :]
        square = phase * phase
        cosine = horner(COS, square)
        sine = horner(SINC, square) * phase
        rough = pl.reciprocal(phase, approx=True)
        gains[k] = rough * (2.0 * gain - (gain * phase) * rough)
        cell[k] = [
            sr * cosine - si * sine,
            sr * sine + si * cosine,
            rr * cosine + ri * sine,
            ri * cosine - rr * sine,
        ]

    for k in (n - 2, n - 1, 0, 1):
        turn(k)
    cell[-1], cell[-2] = [below(v) for v in cell[n - 1]], [below(v) for v in cell[n - 2]]
    cell[n], cell[n + 1] = [above(v) for v in cell[0]], [above(v) for v in cell[1]]
    slope, bend = {}, {}

    def slope_of(k):
        slope[k] = [b - a for a, b in zip(cell[k], cell[k + 1])]

    def bend_of(k):
        bend[k] = [b - a for a, b in zip(slope[k - 1], slope[k])]

    for k in (-2, -1, 0):
        slope_of(k)
    for k in (-1, 0):
        bend_of(k)
    for k in range(n):
        if k + 2 not in cell:
            turn(k + 2)
        slope_of(k + 1)
        bend_of(k + 1)
        curve = [14.0 * e - (a + b) for a, e, b in zip(bend[k - 1], bend[k], bend[k + 1])]
        g = gains[k]
        new = [
            cell[k][0] + g * (damping * curve[0] - curve[1]),
            cell[k][1] + g * (damping * curve[1] + curve[0]),
            cell[k][2] + g * (damping * curve[2] + curve[3]),
            cell[k][3] + g * (damping * curve[3] - curve[2]),
        ]
        for c in range(4):
            state[c, k * SUB : (k + 1) * SUB, :] = new[c]
        products[k * SUB : (k + 1) * SUB, :] = new[0] * new[2] + new[1] * new[3]


def add_contribution(shape, l, products, totals):
    picked = jnp.where(
        iota((LANES, LANES), 1) == l * shape.parts + iota((LANES, LANES), 0) // shape.rows, 1.0, 0.0
    ).astype(jnp.bfloat16)
    pieces = jnp.concatenate(pieces_of(products[...], 2), axis=1)
    totals[...] += jnp.dot(pieces, jnp.concatenate([picked] * 2, axis=0), preferred_element_type=jnp.float32)


def image_of(shape, totals, image):
    for b in range(shape.cells // LANES):
        image[:, b * LANES : (b + 1) * LANES] = turned_back(shape, totals, b)[0 : image.shape[0], :]


def hear(t, records, receiver_pos, heard, hits, planes, sem):
    freqs, width = planes.shape[1:]
    receivers = records.shape[3]
    copy = pltpu.make_async_copy(records.at[t], heard, sem)
    copy.start()
    places = receiver_pos[...]
    for r in range(0, receivers, LANES):
        column = as_column(places[:, r : r + LANES].astype(jnp.float32)).astype(jnp.int32)
        hits[r : r + LANES, :] = jnp.where(iota((LANES, width), 1) == column, 1.0, 0.0).astype(jnp.bfloat16)
    copy.wait()
    pieces = jnp.concatenate([piece for c in range(2) for piece in pieces_of(heard[c], 3)], axis=0)
    for x in range(0, width, 512):
        found = jnp.dot(pieces, hits[:, x : x + 512], preferred_element_type=jnp.float32)
        for c in range(2):
            part = [found[(3 * c + i) * freqs : (3 * c + i + 1) * freqs] for i in range(3)]
            planes[c, :, x : x + 512] = part[0] + part[1] + part[2]


def surface_field(shape, t, f0, wavelet, source_pos, planes, flat, state):
    rows = shape.rows
    for c in range(4):
        if c < 2:
            strength = as_column(wavelet[t, c : c + 1, :])[f0 : f0 + rows]

            def natural(x, strength=strength):
                return jnp.where(iota((rows, LANES), 1) == source_pos[0] - x, strength, 0.0)
        else:
            def natural(x, c=c):
                return planes[c - 2, f0 : f0 + rows, x : x + LANES]
        load_field(shape, natural, c, flat, state)


def run_layers(shape, first, last, w_row, state, slowness, spread_a, spread_b, products, totals):
    layer_slowness(shape, 2 * first, slowness, spread_a)

    def step(i, carry):
        l = 2 * i
        layer_slowness(shape, l + 1, slowness, spread_b)
        layer_step(shape, state, w_row, spread_a, products)
        add_contribution(shape, l, products, totals)
        layer_slowness(shape, l + 2, slowness, spread_a)
        layer_step(shape, state, w_row, spread_b, products)
        add_contribution(shape, l + 1, products, totals)
        return carry

    lax.fori_loop(first, last, step, 0)


def main_kernel(
    shape, chunk, devices, last_chunk,
    fields, angular, surface_angular, wavelet, records, source_pos, receiver_pos,
    model0, model1, model2, *rest,
):
    if last_chunk:
        earlier, planes, sent, own, next1, next2, up, *scratch = rest
    else:
        sent, partial, planes, *scratch = rest
    state, spread_a, spread_b, products, totals, slowness, flat, image, heard, hits, sem = scratch
    rows, parts = shape.rows, shape.parts
    f0 = chunk * rows
    count = LAYERS * TICKS
    d = lax.axis_index("depth")
    end = d == devices - 1

    @pl.when(jnp.logical_not(end))
    def _():
        for c in range(4):
            load_field(shape, lambda x, c=c: fields[0, c, :, x : x + LANES], c, flat, state)

    @pl.when(end)
    def _():
        if not last_chunk:
            hear(0, records, receiver_pos, heard, hits, planes, sem)
        surface_field(shape, 0, f0, wavelet, source_pos, planes, flat, state)

    load_slowness(shape, (model0, model1, model2), flat, slowness)
    w_own = repeated(as_column(angular[...])[f0 : f0 + rows])
    w_top = repeated(as_column(surface_angular[0:1, :])[f0 : f0 + rows])
    w_row = jnp.broadcast_to(jnp.where(end, w_top, w_own), (SUB, LANES))
    totals[...] = jnp.zeros(totals.shape, jnp.float32)
    run_layers(shape, jnp.where(end, LAYERS // 2, 0), count // 2, w_row, state, slowness, spread_a, spread_b, products, totals)
    for c in range(4):
        def put(x, value, c=c):
            sent[c * rows : (c + 1) * rows, x : x + LANES] = value
        store_field(shape, c, state, put)
    if not last_chunk:
        image_of(shape, totals, partial)
        return
    image_of(shape, totals, image)
    scale = 1.0 / math.sqrt(angular.shape[1])
    found = []
    for l in range(count):
        at = pl.ds(l * parts, parts)
        value = (image[at, :] + earlier[at, :]) * scale
        if l >= 2 * LAYERS:
            value = jnp.where(d == devices - 2, 0.0, value)
        found.append(value)

    def filtered(l):
        total = jnp.zeros_like(found[0])
        if 0 <= l < count:
            total = 2.0 * found[l]
        if l >= 1:
            total = total - 0.5 * found[l - 1]
        if l + 1 < count:
            after = found[l + 1]
            total = total - 0.5 * (jnp.where(end, 0.0, after) if l == LAYERS - 1 else after)
        return total

    up[...] = filtered(-1)
    for t, out in enumerate((own, next1, next2)):
        for l in range(LAYERS):
            out[l * parts : (l + 1) * parts, :] = filtered(t * LAYERS + l)
    sent[4 * rows : 4 * rows + parts, 0 : shape.cells] = filtered(count)


def rest_kernel(
    shape, freqs, devices,
    up, fields, angular, surface_angular, wavelet, records, source_pos, receiver_pos, model, model_above,
    sent, extra, out,
    state, spread_a, spread_b, products, totals, slowness, flat, image, heard, hits, planes, held, sem,
):
    rows, parts = shape.rows, shape.parts
    d = lax.axis_index("depth")
    end = d == devices - 1
    top = d == 1
    sent[...] = jnp.zeros(sent.shape, jnp.float32)
    sent[(LAYERS - 1) * parts : LAYERS * parts, :] = up[...]
    extra[...] = jnp.zeros(extra.shape, jnp.float32)

    def keep(f0):
        for c in range(4):
            def put(x, value, c=c):
                out[0, c, f0 : f0 + rows, x : x + LANES] = value
            store_field(shape, c, state, put)

    @pl.when(d == 0)
    def _():
        hear(2, records, receiver_pos, heard, hits, planes, sem)
        for f0 in range(0, freqs, rows):
            surface_field(shape, 2, f0, wavelet, source_pos, planes, flat, state)
            keep(f0)

    @pl.when(jnp.logical_or(top, end))
    def _():
        @pl.when(top)
        def _():
            hear(1, records, receiver_pos, heard, hits, planes, sem)

        @pl.when(end)
        def _():
            copy = pltpu.make_async_copy(fields.at[0], held, sem)
            copy.start()
            copy.wait()

        totals[...] = jnp.zeros(totals.shape, jnp.float32)
        picked = jnp.where(top, model_above[...], model[...])
        load_slowness(shape, (picked,), flat, slowness)
        for f0 in range(0, freqs, rows):
            @pl.when(top)
            def _():
                surface_field(shape, 1, f0, wavelet, source_pos, planes, flat, state)

            @pl.when(end)
            def _():
                for c in range(4):
                    load_field(shape, lambda x, c=c: held[c, f0 : f0 + rows, x : x + LANES], c, flat, state)

            w_own = repeated(as_column(angular[...])[f0 : f0 + rows])
            w_top = repeated(as_column(surface_angular[1:2, :])[f0 : f0 + rows])
            w_row = jnp.broadcast_to(jnp.where(top, w_top, w_own), (SUB, LANES))
            run_layers(shape, 0, LAYERS // 2, w_row, state, slowness, spread_a, spread_b, products, totals)

            @pl.when(top)
            def _():
                keep(f0)
        image_of(shape, totals, image)
        scale = 1.0 / math.sqrt(freqs)
        found = [image[l * parts : (l + 1) * parts, :] * scale for l in range(LAYERS)]
        rows_of = []
        for l in range(LAYERS):
            total = 2.0 * found[l]
            if l > 0:
                total = total - 0.5 * found[l - 1]
            if l + 1 < LAYERS:
                total = total - 0.5 * found[l + 1]
            rows_of.append(total)

        @pl.when(top)
        def _():
            for l in range(LAYERS):
                sent[l * parts : (l + 1) * parts, :] = rows_of[l] + up[...] if l == LAYERS - 1 else rows_of[l]
            extra[0:parts, :] = -0.5 * found[LAYERS - 1]

        @pl.when(end)
        def _():
            for l in range(LAYERS):
                extra[l * parts : (l + 1) * parts, :] = rows_of[l]
            sent[(LAYERS - 1) * parts : LAYERS * parts, :] = -0.5 * found[0]


def slowness_kernel(table, index, out):
    layers, width = index.shape
    levels = table.shape[1]
    cells = out.shape[1]
    parts = width // cells
    number = index[...]
    speed = jnp.broadcast_to(table[:, 0:1], number.shape)
    for n in range(1, levels):
        speed = jnp.where(number == n, table[:, n : n + 1], speed)
    slow = depth_step / speed
    for l in range(layers):
        for q in range(parts):
            out[l * parts + q : l * parts + q + 1, :] = slow[l : l + 1, q * cells : (q + 1) * cells]


def close_kernel(
    first, relayed, second, tail, top, own, from1, from2, below, extra, section, fields_out, sems,
):
    d = lax.axis_index("depth")
    rows = relayed.shape[0] // 4

    def move(source, base, start, count, slot):
        return [
            pltpu.make_async_copy(
                source.at[pl.ds(c * base, count), :],
                fields_out.at[0, c, pl.ds(start, count), :],
                sems.at[slot + c],
            )
            for c in range(4)
        ]

    def run(copies):
        for copy in copies:
            copy.start()

    local = d < 2
    is_relayed = jnp.logical_and(d % 4 == 1, d > 1)

    @pl.when(local)
    def _():
        run([pltpu.make_async_copy(top.at[0, c, pl.ds(0, rows), :], fields_out.at[0, c, pl.ds(0, rows), :], sems.at[c]) for c in range(4)])
        run([pltpu.make_async_copy(top.at[0, c, pl.ds(rows, rows), :], fields_out.at[0, c, pl.ds(rows, rows), :], sems.at[4 + c]) for c in range(4)])

    @pl.when(jnp.logical_not(local))
    def _():
        run(move(second, rows, rows, rows, 4))

        @pl.when(is_relayed)
        def _():
            run(move(relayed, rows, 0, rows, 0))

        @pl.when(jnp.logical_not(is_relayed))
        def _():
            run(move(first, rows, 0, rows, 0))

    parts, cells = extra.shape[0] // LAYERS, extra.shape[1]
    total = own[...] + from1[...] + from2[...] + below[...] + extra[...]
    for l in range(LAYERS):
        rows_of = total[l * parts : (l + 1) * parts, :]
        if l == 0:
            rows_of = rows_of + tail[0:parts, 0:cells]
        for q in range(parts):
            section[l : l + 1, q * cells : (q + 1) * cells] = rows_of[q : q + 1, :]
    for copy in move(first, rows, 0, rows, 0) + move(second, rows, rows, rows, 4):
        copy.wait()


VMEM = pl.BlockSpec(memory_space=pltpu.VMEM)
SMEM = pl.BlockSpec(memory_space=pltpu.SMEM)
HBM = pl.BlockSpec(memory_space=pltpu.HBM)
ANY = pl.BlockSpec(memory_space=pl.ANY)
PARAMS = pltpu.CompilerParams(vmem_limit_bytes=40 * 2**20)


def f32(*shape):
    return jax.ShapeDtypeStruct(shape, jnp.float32)


def scratch_of(shape, receivers, freqs, count):
    square = pltpu.VMEM((SUB * shape.steps, LANES), jnp.float32)
    return [
        pltpu.VMEM((4, SUB * shape.steps, LANES), jnp.float32),
        square,
        square,
        square,
        square,
        pltpu.VMEM((SUB * shape.steps, 3 * LANES), jnp.bfloat16),
        square,
        pltpu.VMEM((count * shape.parts, shape.cells), jnp.float32),
        pltpu.VMEM((2, freqs, receivers), jnp.float32),
        pltpu.VMEM((receivers, shape.width), jnp.bfloat16),
    ]


def on_device(
    devices,
    fields_in, flight_angular, wavelet, surface_angular, records, source_pos, receiver_pos, vel_table, vel_index,
):
    width = fields_in.shape[3]
    freqs = fields_in.shape[2]
    receivers = records.shape[3]
    rows = freqs // 2
    shape = Shape(rows, width)
    parts, cells, count = shape.parts, shape.cells, LAYERS * TICKS
    axis = "depth"
    positions = receiver_pos.reshape(1, receivers)
    near = f32(LAYERS * parts, cells)
    model = pl.pallas_call(
        slowness_kernel,
        out_shape=near,
        in_specs=[VMEM, VMEM],
        out_specs=VMEM,
        compiler_params=PARAMS,
        name="slowness",
    )(vel_table, vel_index)
    last = devices - 1
    model1 = lax.ppermute(model, axis, [(i, (i - 1) % devices) for i in range(devices)])
    model2 = lax.ppermute(model, axis, [(i, (i - 2) % devices) for i in range(devices)])
    model_above = lax.ppermute(model, axis, [(0, 1)])

    def main(chunk, earlier, planes):
        last_chunk = earlier is not None
        ins = [fields_in, flight_angular, surface_angular, wavelet, records, source_pos, positions, model, model1, model2]
        specs = [
            pl.BlockSpec((1, 4, rows, width), lambda i: (0, 0, chunk, 0)),
            VMEM, VMEM, VMEM, HBM, SMEM, VMEM, VMEM, VMEM, VMEM,
        ]
        if last_chunk:
            ins += [earlier, planes]
            specs += [VMEM, VMEM]
            outs = (f32(4 * rows + SUB, width), near, near, near, f32(parts, cells))
        else:
            outs = (f32(4 * rows, width), f32(count * parts, cells), f32(2, freqs, width))

        def body(*refs):
            main_kernel(shape, chunk, devices, last_chunk, *refs)

        return pl.pallas_call(
            body,
            grid=(1,),
            out_shape=outs,
            in_specs=specs,
            out_specs=[VMEM] * len(outs),
            scratch_shapes=scratch_of(shape, receivers, freqs, count) + [pltpu.SemaphoreType.DMA],
            compiler_params=PARAMS,
            name="blocks",
        )(*ins)

    on = [(i, i + 3) for i in range(devices - 3)]
    direct = on + [(last, 2)]
    via = [(i, i - 1) if i % 4 == 2 else (i, j) for i, j in on] + [(last, 2)]
    relay = [(i, i + 4) for i in range(1, devices - 4, 4)]

    sent1, partial, planes = main(0, None, None)
    first = lax.ppermute(sent1, axis, via)
    sent2, own, next1, next2, up = main(1, partial, planes)
    second = lax.ppermute(sent2, axis, direct)
    relayed = lax.ppermute(first, axis, relay)
    from1 = lax.ppermute(next1, axis, [(i, (i + 1) % devices) for i in range(devices)])
    from2 = lax.ppermute(next2, axis, [(i, i + 2) for i in range(devices - 2)] + [(last, 1)])
    sent_up, extra, top = pl.pallas_call(
        lambda *refs: rest_kernel(shape, freqs, devices, *refs),
        out_shape=(near, near, f32(1, 4, freqs, width)),
        in_specs=[VMEM, HBM, VMEM, VMEM, VMEM, HBM, SMEM, VMEM, VMEM, VMEM],
        out_specs=[VMEM] * 3,
        scratch_shapes=scratch_of(shape, receivers, freqs, LAYERS)
        + [
            pltpu.VMEM((2, freqs, width), jnp.float32),
            pltpu.VMEM((4, freqs, width), jnp.float32),
            pltpu.SemaphoreType.DMA,
        ],
        compiler_params=PARAMS,
        name="rest",
    )(up, fields_in, flight_angular, surface_angular, wavelet, records, source_pos, positions, model, model_above)
    below = lax.ppermute(sent_up, axis, [(i, i - 1) for i in range(1, devices)])
    section, fields_out = pl.pallas_call(
        close_kernel,
        grid=(1,),
        out_shape=(f32(LAYERS, width), f32(1, 4, freqs, width)),
        in_specs=[ANY, ANY, ANY, pl.BlockSpec((SUB, width), lambda i: (4 * rows // SUB, 0)), ANY, VMEM, VMEM, VMEM, VMEM, VMEM],
        out_specs=[VMEM, ANY],
        scratch_shapes=[pltpu.SemaphoreType.DMA((8,))],
        compiler_params=PARAMS,
        name="close",
    )(first, relayed, second, second, top, own, from1, from2, below, extra)
    return section, fields_out


def solution(mesh):
    placed = (
        P("depth", None, "shots", None),
        P("depth", "shots"),
        P(None, None, "shots"),
        P(None, "shots"),
        P(None, None, "shots", None),
        P("shots"),
        P("shots"),
        P("depth", None),
        P("depth", None),
    )
    devices = mesh.shape["depth"]

    def run(*args):
        return on_device(devices, *args)

    return jax.shard_map(
        run,
        mesh=mesh,
        in_specs=placed,
        out_specs=(P("depth", "shots"), P("depth", None, "shots", None)),
        check_vma=False,
    )
```

time: 63.6 us -> 53.5 us (0.84)
  Pallas kernels: 32 us -> 24 us
  local copies, waits for them, and re-layouts: 2.39 us -> 3.8 us
  waiting for transfers between devices: 6.32 us -> 5.01 us
  starting transfers between devices: 19.9 us -> 18.7 us
  other arithmetic: 0.89 us -> 0 us
    pallas_call x2, Pallas kernels: 21 us -> 13.7 us  [main(): pl.pallas_call(body, grid=(1,), out_shape=outs, in_specs=specs, out_specs...]
    ppermute x1, starting transfers between devices: 7.02 us -> 5.16 us  [on_device(): lax.ppermute(model, axis, [(i, (i - 2) % devices) for i in range(devices)])]
    unnamed x16, local copies, waits for them, and re-layouts: 2.39 us -> 3.8 us
    ppermute x1, starting transfers between devices: 0.06 us -> 0.96 us  [on_device(): lax.ppermute(model, axis, [(i, (i - 1) % devices) for i in range(devices)])]
    concatenate x2 -> x0, other arithmetic: 0.89 us -> none  [the longest x1 0.87 us: on_device(): jnp.concatenate([vel_table] * 3, axis=1)]
    ppermute x1, waiting for transfers between devices: 2.43 us -> 1.71 us  [on_device(): lax.ppermute(model, axis, [(i, (i - 1) % devices) for i in range(devices)])]
    pallas_call x2 -> x3, Pallas kernels: 11 us -> 10.3 us  [the longest x1 8.54 us: on_device(): pl.pallas_call(lambda *refs: rest_kernel(shape, freqs, devices, *refs), o...]
  transfers between devices with their start and end apart: 9 -> 9, of which waited for: 3 -> 2; matrix products, arithmetic and copies ran while one was open for 0% -> 0% of each run, Pallas kernels for 32% -> 29%
where the time goes in v1:
time: 53.5 us; the launch traced here: 53.1 us
  Pallas kernels  24 us (45%)
  starting transfers between devices  18.7 us (35%)
  waiting for transfers between devices  5.01 us (9%)
  local copies, waits for them, and re-layouts  3.8 us (7%)
  between operations  1.64 us (3%)
    pallas_call x2, Pallas kernels, main(): pl.pallas_call(body, grid=(1,), out_shape=outs, in_specs=specs, out_specs...  13.7 us
    pallas_call x1, Pallas kernels, on_device(): pl.pallas_call(lambda *refs: rest_kernel(shape, freqs, devices, *refs), o...  8.54 us
    ppermute x1, starting transfers between devices, on_device(): lax.ppermute(model, axis, [(i, (i - 2) % devices) for i in range(devices)])  5.16 us
    unnamed x16, local copies, waits for them, and re-layouts  3.8 us
    ppermute x1, waiting for transfers between devices, on_device(): below = lax.ppermute(sent_up, axis, [(i, i - 1) for i in range(1, devices)])  3.28 us
    ppermute x1, starting transfers between devices, on_device(): relayed = lax.ppermute(first, axis, relay)  3.2 us
    ppermute x1, starting transfers between devices, on_device(): second = lax.ppermute(sent2, axis, direct)  2.28 us
    ppermute x1, starting transfers between devices, on_device(): first = lax.ppermute(sent1, axis, via)  1.92 us
  transfers between devices with their start and end apart: 9, of which 2 were waited for; matrix products, arithmetic and copies ran while one was open for 0% of the time, Pallas kernels for 29%

profile of v1, /device:TPU:1, one launch (start us, length us, event | category | flops | bytes accessed | tf_op | source)
XLA Modules:
  0.0 53.1 jit_solution(5773408804909329260)
XLA Ops:
  0.6 0.0 copy-start.3
  0.6 0.7 %copy-done.3 = s32[4,2048]{1,0:T(4,128)S(1)} copy-done((s32[4,2048]{1,0:T(4,128)S(1)}, s32[4,2048]{1,0:T(4,128)}, u32[]{:S(2)}) %copy-start.3) | copy-done | bytes 32792
  1.4 0.0 copy-start.7
  1.4 0.7 %copy-done.7 = f32[4,16]{1,0:T(4,128)S(1)} copy-done((f32[4,16]{1,0:T(4,128)S(1)}, f32[4,16]{1,0:T(4,128)}, u32[]{:S(2)}) %copy-start.7) | copy-done | bytes 280
  2.1 0.0 copy-start.2
  2.1 0.0 copy-start.5
  2.1 0.1 slowness.1.refs_7_.refs_8_
  2.2 0.0 copy-start.4
  2.2 5.2 %collective-permute-start.1 = (f32[32,256]{1,0:T(8,128)S(1)}, f32[32,256]{1,0:T(8,128)S(1)}, u32[]{:S(2)}, u32[]{:S(2)}) collective-permute-start(f32[32,256]{1,0:T(8,128)S(1)} %slowness.1.refs_7_.refs_8_), channel_id=1, source_target_pairs={{0,14},{1,15},{2,0},{3,1},{4,2},{5,3},{6,4},{7,5},{8,6},{9,7},{10,... | collective-permute-start | bytes 98312 | tf_op jit(solution)/shard_map/ppermute | solution.py:503
  7.4 1.0 %collective-permute-start = (f32[32,256]{1,0:T(8,128)S(1)}, f32[32,256]{1,0:T(8,128)S(1)}, u32[]{:S(2)}, u32[]{:S(2)}) collective-permute-start(f32[32,256]{1,0:T(8,128)S(1)} %slowness.1.refs_7_.refs_8_), channel_id=1, source_target_pairs={{0,15},{1,0},{2,1},{3,2},{4,3},{5,4},{6,5},{7,6},{8,7},{9,8},{10,9... | collective-permute-start | bytes 98312 | tf_op jit(solution)/shard_map/ppermute | solution.py:502
  9.0 0.0 copy-start.6
  9.0 0.0 collective-permute-done.1.refs_9_
  9.0 1.7 %collective-permute-done.refs_8_ = f32[32,256]{1,0:T(8,128)S(1)} collective-permute-done((f32[32,256]{1,0:T(8,128)S(1)}, f32[32,256]{1,0:T(8,128)S(1)}, u32[]{:S(2)}, u32[]{:S(2)}) %collective-permute-start) | collective-permute-done | bytes 32800 | tf_op jit(solution)/shard_map/ppermute | solution.py:502
  10.7 0.0 copy-done.2
  10.7 0.0 copy-done.5
  10.7 0.0 copy-done.4
  10.7 0.0 copy-done.6
  10.7 0.0 copy-start
  10.7 1.2 %copy-done = f32[1,4,32,2048]{3,2,1,0:T(8,128)S(1)} copy-done((f32[1,4,32,2048]{3,2,1,0:T(8,128)S(1)}, f32[1,4,32,2048]{3,2,1,0:T(8,128)}, u32[]{:S(2)}) %copy-start) | copy-done | bytes 1048600
  12.0 0.0 copy-start.1
  12.0 1.1 %copy-done.1 = f32[3,2,32,1024]{3,2,1,0:T(8,128)S(1)} copy-done((f32[3,2,32,1024]{3,2,1,0:T(8,128)S(1)}, f32[3,2,32,1024]{3,2,1,0:T(8,128)}, u32[]{:S(2)}) %copy-start.1) | copy-done | bytes 786456
  13.1 6.8 %blocks.2 = (f32[64,2048]{1,0:T(8,128)S(1)}, f32[96,256]{1,0:T(8,128)S(1)}, f32[2,32,2048]{2,1,0:T(8,128)S(1)}) custom-call(f32[1,4,32,2048]{3,2,1,0:T(8,128)S(1)} %copy-done, f32[1,32]{1,0:T(1,128)S(1)} %copy-done.6, f32[3,32]{1,0:T(4,128)S(1)} %copy-done.5, f32[3,2,32]{2,1,0:T(2,128)S(1)} %copy-done.4, f32[3,2,32,1024]{3,2,1,0:T(8,128)S(1)} %copy-done.1, ...), custom_call_target="tpu_custom_call" | custom-call | tf_op jit(solution)/shard_map/blocks/pallas_call | solution.py:523
  19.9 1.9 %collective-permute-start.2 = (f32[64,2048]{1,0:T(8,128)S(1)}, f32[64,2048]{1,0:T(8,128)S(1)}, u32[]{:S(2)}, u32[]{:S(2)}) collective-permute-start(f32[64,2048]{1,0:T(8,128)S(1)} %get-tuple-element.13), channel_id=1, source_target_pairs={{0,3},{1,4},{2,1},{3,6},{4,7},{5,8},{6,5},{7,10},{8,11},{9,12},{10... | collective-permute-start | bytes 1572872 | tf_op jit(solution)/shard_map/ppermute | solution.py:540
  21.8 6.8 %blocks.3 = (f32[72,2048]{1,0:T(8,128)S(1)}, f32[32,256]{1,0:T(8,128)S(1)}, f32[32,256]{1,0:T(8,128)S(1)}, f32[32,256]{1,0:T(8,128)S(1)}, f32[8,256]{1,0:T(8,128)S(1)}) custom-call(f32[1,4,32,2048]{3,2,1,0:T(8,128)S(1)} %copy-done, f32[1,32]{1,0:T(1,128)S(1)} %copy-done.6, f32[3,32]{1,0:T(4,128)S(1)} %copy-done.5, f32[3,2,32]{2,1,0:T(2,128)S(1)} %copy-done.4, ...), custom_call_target="tpu_custom_call" | custom-call | tf_op jit(solution)/shard_map/blocks/pallas_call | solution.py:523
  28.7 2.3 %collective-permute-start.4 = (f32[72,2048]{1,0:T(8,128)S(1)}, f32[72,2048]{1,0:T(8,128)S(1)}, u32[]{:S(2)}, u32[]{:S(2)}) collective-permute-start(f32[72,2048]{1,0:T(8,128)S(1)} %get-tuple-element.16), channel_id=1, source_target_pairs={{0,3},{1,4},{2,5},{3,6},{4,7},{5,8},{6,9},{7,10},{8,11},{9,12},{10... | collective-permute-start | bytes 1769480 | tf_op jit(solution)/shard_map/ppermute | solution.py:542
  31.0 0.0 collective-permute-done.2.first
  31.0 3.2 %collective-permute-start.3 = (f32[64,2048]{1,0:T(8,128)S(1)}, f32[64,2048]{1,0:T(8,128)S(1)}, u32[]{:S(2)}, u32[]{:S(2)}) collective-permute-start(f32[64,2048]{1,0:T(8,128)S(1)} %collective-permute-done.2.first), channel_id=1, source_target_pairs={{1,5},{5,9},{9,13},{17,21},{21,25},{25,29}} | collective-permute-start | bytes 1572872 | tf_op jit(solution)/shard_map/ppermute | solution.py:543
  34.2 1.3 %collective-permute-start.5 = (f32[32,256]{1,0:T(8,128)S(1)}, f32[32,256]{1,0:T(8,128)S(1)}, u32[]{:S(2)}, u32[]{:S(2)}) collective-permute-start(f32[32,256]{1,0:T(8,128)S(1)} %slowness.1.refs_7_.refs_8_), channel_id=1, source_target_pairs={{0,1},{16,17}} | collective-permute-start | bytes 98312 | tf_op jit(solution)/shard_map/ppermute | solution.py:504
  35.5 0.1 collective-permute-start.6
  35.6 1.9 %collective-permute-start.7 = (f32[32,256]{1,0:T(8,128)S(1)}, f32[32,256]{1,0:T(8,128)S(1)}, u32[]{:S(2)}, u32[]{:S(2)}) collective-permute-start(f32[32,256]{1,0:T(8,128)S(1)} %get-tuple-element.21), channel_id=1, source_target_pairs={{0,2},{1,3},{2,4},{3,5},{4,6},{5,7},{6,8},{7,9},{8,10},{9,11},{10,... | collective-permute-start | bytes 98312 | tf_op jit(solution)/shard_map/ppermute | solution.py:545
  37.5 0.0 collective-permute-done.5.refs_9_
  37.5 8.5 %rest.1 = (f32[32,256]{1,0:T(8,128)S(1)}, f32[32,256]{1,0:T(8,128)S(1)}, f32[1,4,32,2048]{3,2,1,0:T(8,128)S(1)}) custom-call(f32[8,256]{1,0:T(8,128)S(1)} %get-tuple-element.17.refs_0_, f32[1,4,32,2048]{3,2,1,0:T(8,128)S(1)} %copy-done, f32[1,32]{1,0:T(1,128)S(1)} %copy-done.6, f32[3,32]{1,0:T(4,128)S(1)} %copy-done.5, f32[3,2,32]{2,1,0:T(2,128)S(1)} %copy-done.4, ...), custom_call_target="tpu_custom_call" | custom-call | tf_op jit(solution)/shard_map/rest/pallas_call | solution.py:546
  46.0 1.9 %collective-permute-start.8 = (f32[32,256]{1,0:T(8,128)S(1)}, f32[32,256]{1,0:T(8,128)S(1)}, u32[]{:S(2)}, u32[]{:S(2)}) collective-permute-start(f32[32,256]{1,0:T(8,128)S(1)} %get-tuple-element.22), channel_id=1, source_target_pairs={{1,0},{2,1},{3,2},{4,3},{5,4},{6,5},{7,6},{8,7},{9,8},{10,9},{11,1... | collective-permute-start | bytes 98312 | tf_op jit(solution)/shard_map/ppermute | solution.py:560
  48.0 0.0 collective-permute-done.6.from1
  48.0 0.0 collective-permute-done.7.from2
  48.0 3.3 %collective-permute-done.8.below = f32[32,256]{1,0:T(8,128)S(1)} collective-permute-done((f32[32,256]{1,0:T(8,128)S(1)}, f32[32,256]{1,0:T(8,128)S(1)}, u32[]{:S(2)}, u32[]{:S(2)}) %collective-permute-start.8) | collective-permute-done | bytes 32800 | tf_op jit(solution)/shard_map/ppermute | solution.py:560
  51.3 0.0 collective-permute-done.4.second.tail
  51.3 0.0 collective-permute-done.3.relayed
  51.3 1.7 %close.1 = (f32[4,2048]{1,0:T(4,128)}, f32[1,4,32,2048]{3,2,1,0:T(8,128)}) custom-call(f32[64,2048]{1,0:T(8,128)S(1)} %collective-permute-done.2.first, f32[64,2048]{1,0:T(8,128)S(1)} %collective-permute-done.3.relayed, f32[72,2048]{1,0:T(8,128)S(1)} %collective-permute-done.4.second.tail, f32[72,2048]{1,0:T(8,128)S(1)} %collective-permute-done.4.second.tail, ...), custom_call_target="tpu_custom_call" | custom-call | tf_op jit(solution)/shard_map/close/pallas_call | solution.py:561
Async XLA Ops:
  0.6 0.8 %copy-start.3 = (s32[4,2048]{1,0:T(4,128)S(1)}, s32[4,2048]{1,0:T(4,128)}, u32[]{:S(2)}) copy-start(s32[4,2048]{1,0:T(4,128)} %index.1) | copy-start | bytes 98308
  1.4 0.7 %copy-start.7 = (f32[4,16]{1,0:T(4,128)S(1)}, f32[4,16]{1,0:T(4,128)}, u32[]{:S(2)}) copy-start(f32[4,16]{1,0:T(4,128)} %table.1) | copy-start | bytes 772
  2.1 8.6 %copy-start.2 = (s32[1024]{0:T(1024)S(1)}, s32[1024]{0:T(1024)}, u32[]{:S(2)}) copy-start(s32[1024]{0:T(1024)} %param.15) | copy-start | bytes 12292
  2.1 8.6 %copy-start.5 = (f32[3,32]{1,0:T(4,128)S(1)}, f32[3,32]{1,0:T(4,128)}, u32[]{:S(2)}) copy-start(f32[3,32]{1,0:T(4,128)} %refs_3_.5) | copy-start | bytes 1156
  2.2 8.5 %copy-start.4 = (f32[3,2,32]{2,1,0:T(2,128)S(1)}, f32[3,2,32]{2,1,0:T(2,128)}, u32[]{:S(2)}) copy-start(f32[3,2,32]{2,1,0:T(2,128)} %refs_4_.5) | copy-start | bytes 2308
  2.2 6.8 %collective-permute-start.1 = (f32[32,256]{1,0:T(8,128)S(1)}, f32[32,256]{1,0:T(8,128)S(1)}, u32[]{:S(2)}, u32[]{:S(2)}) collective-permute-start(f32[32,256]{1,0:T(8,128)S(1)} %slowness.1.refs_7_.refs_8_), channel_id=1, source_target_pairs={{0,14},{1,15},{2,0},{3,1},{4,2},{5,3},{6,4},{7,5},{8,6},{9,7},{10,... | collective-permute-start | bytes 98312 | tf_op jit(solution)/shard_map/ppermute | solution.py:503
  7.4 3.3 %collective-permute-start = (f32[32,256]{1,0:T(8,128)S(1)}, f32[32,256]{1,0:T(8,128)S(1)}, u32[]{:S(2)}, u32[]{:S(2)}) collective-permute-start(f32[32,256]{1,0:T(8,128)S(1)} %slowness.1.refs_7_.refs_8_), channel_id=1, source_target_pairs={{0,15},{1,0},{2,1},{3,2},{4,3},{5,4},{6,5},{7,6},{8,7},{9,8},{10,9... | collective-permute-start | bytes 98312 | tf_op jit(solution)/shard_map/ppermute | solution.py:502
  9.0 1.7 %copy-start.6 = (f32[1,32]{1,0:T(1,128)S(1)}, f32[1,32]{1,0:T(1,128)}, u32[]{:S(2)}) copy-start(f32[1,32]{1,0:T(1,128)} %refs_2_.5) | copy-start | bytes 388
  10.7 1.2 %copy-start = (f32[1,4,32,2048]{3,2,1,0:T(8,128)S(1)}, f32[1,4,32,2048]{3,2,1,0:T(8,128)}, u32[]{:S(2)}) copy-start(f32[1,4,32,2048]{3,2,1,0:T(8,128)} %refs_1_.5) | copy-start | bytes 3145732
  12.0 1.1 %copy-start.1 = (f32[3,2,32,1024]{3,2,1,0:T(8,128)S(1)}, f32[3,2,32,1024]{3,2,1,0:T(8,128)}, u32[]{:S(2)}) copy-start(f32[3,2,32,1024]{3,2,1,0:T(8,128)} %refs_5_.3) | copy-start | bytes 2359300
  19.9 11.1 %collective-permute-start.2 = (f32[64,2048]{1,0:T(8,128)S(1)}, f32[64,2048]{1,0:T(8,128)S(1)}, u32[]{:S(2)}, u32[]{:S(2)}) collective-permute-start(f32[64,2048]{1,0:T(8,128)S(1)} %get-tuple-element.13), channel_id=1, source_target_pairs={{0,3},{1,4},{2,1},{3,6},{4,7},{5,8},{6,5},{7,10},{8,11},{9,12},{10... | collective-permute-start | bytes 1572872 | tf_op jit(solution)/shard_map/ppermute | solution.py:540
  28.7 22.6 %collective-permute-start.4 = (f32[72,2048]{1,0:T(8,128)S(1)}, f32[72,2048]{1,0:T(8,128)S(1)}, u32[]{:S(2)}, u32[]{:S(2)}) collective-permute-start(f32[72,2048]{1,0:T(8,128)S(1)} %get-tuple-element.16), channel_id=1, source_target_pairs={{0,3},{1,4},{2,5},{3,6},{4,7},{5,8},{6,9},{7,10},{8,11},{9,12},{10... | collective-permute-start | bytes 1769480 | tf_op jit(solution)/shard_map/ppermute | solution.py:542
  31.0 20.3 %collective-permute-start.3 = (f32[64,2048]{1,0:T(8,128)S(1)}, f32[64,2048]{1,0:T(8,128)S(1)}, u32[]{:S(2)}, u32[]{:S(2)}) collective-permute-start(f32[64,2048]{1,0:T(8,128)S(1)} %collective-permute-done.2.first), channel_id=1, source_target_pairs={{1,5},{5,9},{9,13},{17,21},{21,25},{25,29}} | collective-permute-start | bytes 1572872 | tf_op jit(solution)/shard_map/ppermute | solution.py:543
  34.2 3.3 %collective-permute-start.5 = (f32[32,256]{1,0:T(8,128)S(1)}, f32[32,256]{1,0:T(8,128)S(1)}, u32[]{:S(2)}, u32[]{:S(2)}) collective-permute-start(f32[32,256]{1,0:T(8,128)S(1)} %slowness.1.refs_7_.refs_8_), channel_id=1, source_target_pairs={{0,1},{16,17}} | collective-permute-start | bytes 98312 | tf_op jit(solution)/shard_map/ppermute | solution.py:504
  35.5 12.5 %collective-permute-start.6 = (f32[32,256]{1,0:T(8,128)S(1)}, f32[32,256]{1,0:T(8,128)S(1)}, u32[]{:S(2)}, u32[]{:S(2)}) collective-permute-start(f32[32,256]{1,0:T(8,128)S(1)} %get-tuple-element.20), channel_id=1, source_target_pairs={{0,1},{1,2},{2,3},{3,4},{4,5},{5,6},{6,7},{7,8},{8,9},{9,10},{10,1... | collective-permute-start | bytes 98312 | tf_op jit(solution)/shard_map/ppermute | solution.py:544
  35.6 12.4 %collective-permute-start.7 = (f32[32,256]{1,0:T(8,128)S(1)}, f32[32,256]{1,0:T(8,128)S(1)}, u32[]{:S(2)}, u32[]{:S(2)}) collective-permute-start(f32[32,256]{1,0:T(8,128)S(1)} %get-tuple-element.21), channel_id=1, source_target_pairs={{0,2},{1,3},{2,4},{3,5},{4,6},{5,7},{6,8},{7,9},{8,10},{9,11},{10,... | collective-permute-start | bytes 98312 | tf_op jit(solution)/shard_map/ppermute | solution.py:545
  46.0 5.2 %collective-permute-start.8 = (f32[32,256]{1,0:T(8,128)S(1)}, f32[32,256]{1,0:T(8,128)S(1)}, u32[]{:S(2)}, u32[]{:S(2)}) collective-permute-start(f32[32,256]{1,0:T(8,128)S(1)} %get-tuple-element.22), channel_id=1, source_target_pairs={{1,0},{2,1},{3,2},{4,3},{5,4},{6,5},{7,6},{8,7},{9,8},{10,9},{11,1... | collective-permute-start | bytes 98312 | tf_op jit(solution)/shard_map/ppermute | solution.py:560

commit v2 on v1

v2 whole, which is shorter than its diff:
```python
import math

import jax
import jax.numpy as jnp
from jax import lax
from jax.experimental import pallas as pl
from jax.experimental.pallas import tpu as pltpu
from jax.sharding import PartitionSpec as P

TICKS = 3
SUB = 8
LANES = 128
LAYERS = 4
LEVELS = 16

depth_step = 1.0
lateral_scale = 0.03
damping = 0.3


COS = (0.9999999956, -0.4999999227, 0.04166644492, -0.001388656022, 2.469073179e-05, -2.510758575e-07)
SINC = (0.9999999997, -0.1666666607, 0.00833331612, -0.0001983946321, 2.747139839e-06, -2.315705927e-08)


def horner(coefficients, z):
    total = jnp.full(z.shape, coefficients[-1], jnp.float32)
    for c in coefficients[-2::-1]:
        total = total * z + c
    return total


def iota(shape, axis):
    return lax.broadcasted_iota(jnp.int32, shape, axis)


def as_column(row):
    n = row.shape[1]
    return jnp.sum(jnp.where(iota((n, n), 0) == iota((n, n), 1), row, 0.0), axis=1, keepdims=True)


def repeated(column):
    n = column.shape[0]
    return jnp.sum(jnp.where(iota((n, LANES), 0) == iota((n, LANES), 1) % n, column, 0.0), axis=0, keepdims=True)


def pieces_of(value, count):
    found = []
    for i in range(count):
        piece = value.astype(jnp.bfloat16)
        found.append(piece)
        if i + 1 < count:
            value = value - piece.astype(jnp.float32)
    return found


class Shape:
    def __init__(self, rows, width):
        self.rows, self.width = rows, width
        self.parts = LANES // rows
        self.cells = width // self.parts
        self.steps = self.cells // SUB


def load_field(shape, natural, c, flat, state):
    for b in range(shape.cells // LANES):
        stacked = jnp.concatenate(
            [natural(q * shape.cells + b * LANES) for q in range(shape.parts)], axis=0
        )
        flat[b * LANES : (b + 1) * LANES, :] = stacked.T
    for k in range(shape.steps):
        state[c, k * SUB : (k + 1) * SUB, :] = flat[pl.ds(k, SUB, stride=shape.steps), :]


def turned_back(shape, ref, b):
    rows = []
    for x in range(b * LANES, (b + 1) * LANES, SUB):
        sub, k = x // shape.steps, x % shape.steps
        rows.append(ref[pl.ds(k * SUB + sub, SUB, stride=SUB), :])
    return jnp.concatenate(rows, axis=0).T


def store_field(shape, c, state, put):
    for b in range(shape.cells // LANES):
        turned = turned_back(shape, state.at[c], b)
        for q in range(shape.parts):
            put(q * shape.cells + b * LANES, turned[q * shape.rows : (q + 1) * shape.rows, :])


def load_known(shape, models, flat, known):
    parts, count = shape.parts, LAYERS * shape.parts
    for t, model in enumerate(models):
        number = model[0:count, :]
        speeds = []
        for l in range(LAYERS):
            own = number[l * parts : (l + 1) * parts, :]
            table = model[count + l : count + l + 1, 0:LEVELS]
            speed = jnp.broadcast_to(table[:, 0:1], own.shape)
            for n in range(1, LEVELS):
                speed = jnp.where(own == float(n), table[:, n : n + 1], speed)
            speeds.append(jnp.where(speed > 0.0, speed, 1.0))
        rows = [number] + [piece.astype(jnp.float32) for piece in pieces_of(jnp.concatenate(speeds, axis=0), 3)]
        stacked = jnp.concatenate(rows, axis=0)
        for b in range(shape.cells // LANES):
            flat[b * LANES : (b + 1) * LANES, :] = stacked[:, b * LANES : (b + 1) * LANES].T
        for k in range(0, shape.steps, 2):
            pair = [flat[pl.ds(k + i, SUB, stride=shape.steps), :] for i in range(2)]
            known[k * SUB : (k + 2) * SUB, t * LANES : (t + 1) * LANES] = jnp.concatenate(pair, axis=0).astype(jnp.bfloat16)


def layer_tables(shape, l, w_row, speed_row, known, weights, tables, gains):
    count = LAYERS * shape.parts
    row, lane = iota((LANES, 2 * LANES), 0), iota((LANES, 2 * LANES), 1)
    mine = row % count == l * shape.parts + lane % LANES // shape.rows
    chosen = jnp.where(jnp.logical_and(mine, (row < count) == (lane < LANES)), 1.0, 0.0).astype(jnp.bfloat16)
    spread = jnp.dot(known, chosen, preferred_element_type=jnp.float32)
    level = (iota((1, LANES), 1) % LEVELS).astype(jnp.float32)
    hot = jnp.where(spread[:, :LANES] == level, 1.0, 0.0).astype(jnp.bfloat16)
    gains[...] = spread[:, LANES:] * ((lateral_scale / 24.0) / w_row)
    phase = w_row * (depth_step / as_column(jnp.where(speed_row > 0.0, speed_row, 1.0)))
    z = phase * phase
    own = iota((LEVELS, LANES), 1) // shape.rows
    for t, table in enumerate((horner(COS, z), horner(SINC, z) * phase)):
        for i, piece in enumerate(pieces_of(table, 2)):
            piece = piece.astype(jnp.float32)
            for q in range(shape.parts):
                at = (i * shape.parts + q) * LEVELS
                weights[at : at + LEVELS, t * LANES : (t + 1) * LANES] = jnp.where(own == q, piece, 0.0).astype(jnp.bfloat16)
    tables[...] = jnp.dot(jnp.concatenate([hot, hot], axis=1), weights[...], preferred_element_type=jnp.float32)


def layer_step(shape, state, tables, gains, products):
    n = shape.steps
    sub, lane = iota((SUB, LANES), 0), iota((SUB, LANES), 1)
    rows = shape.rows
    cell = {}

    def below(v):
        r = pltpu.roll(v, 1, 0)
        return jnp.where(sub == 0, jnp.where(lane < rows, 0.0, pltpu.roll(r, rows, 1)), r)

    def above(v):
        r = pltpu.roll(v, SUB - 1, 0)
        return jnp.where(sub == SUB - 1, jnp.where(lane >= LANES - rows, 0.0, pltpu.roll(r, LANES - rows, 1)), r)

    def turn(k):
        at = pl.ds(k * SUB, SUB)
        sr, si, rr, ri = (state[c, at, :] for c in range(4))
        cosine, sine = tables[at, 0:LANES], tables[at, LANES : 2 * LANES]
        cell[k] = [
            sr * cosine - si * sine,
            sr * sine + si * cosine,
            rr * cosine + ri * sine,
            ri * cosine - rr * sine,
        ]

    for k in (n - 2, n - 1, 0, 1):
        turn(k)
    cell[-1], cell[-2] = [below(v) for v in cell[n - 1]], [below(v) for v in cell[n - 2]]
    cell[n], cell[n + 1] = [above(v) for v in cell[0]], [above(v) for v in cell[1]]
    slope, bend = {}, {}

    def slope_of(k):
        slope[k] = [b - a for a, b in zip(cell[k], cell[k + 1])]

    def bend_of(k):
        bend[k] = [b - a for a, b in zip(slope[k - 1], slope[k])]

    for k in (-2, -1, 0):
        slope_of(k)
    for k in (-1, 0):
        bend_of(k)
    for k in range(n):
        if k + 2 not in cell:
            turn(k + 2)
        slope_of(k + 1)
        bend_of(k + 1)
        curve = [14.0 * e - (a + b) for a, e, b in zip(bend[k - 1], bend[k], bend[k + 1])]
        g = gains[k * SUB : (k + 1) * SUB, :]
        new = [
            cell[k][0] + g * (damping * curve[0] - curve[1]),
            cell[k][1] + g * (damping * curve[1] + curve[0]),
            cell[k][2] + g * (damping * curve[2] + curve[3]),
            cell[k][3] + g * (damping * curve[3] - curve[2]),
        ]
        for c in range(4):
            state[c, k * SUB : (k + 1) * SUB, :] = new[c]
        products[k * SUB : (k + 1) * SUB, :] = new[0] * new[2] + new[1] * new[3]


def add_contribution(shape, l, products, totals):
    picked = jnp.where(
        iota((LANES, LANES), 1) == l * shape.parts + iota((LANES, LANES), 0) // shape.rows, 1.0, 0.0
    ).astype(jnp.bfloat16)
    pieces = jnp.concatenate(pieces_of(products[...], 2), axis=1)
    totals[...] += jnp.dot(pieces, jnp.concatenate([picked] * 2, axis=0), preferred_element_type=jnp.float32)


def image_of(shape, totals, image):
    for b in range(shape.cells // LANES):
        image[:, b * LANES : (b + 1) * LANES] = turned_back(shape, totals, b)[0 : image.shape[0], :]


def hear(t, records, receiver_pos, heard, hits, planes, sem):
    freqs, width = planes.shape[1:]
    receivers = records.shape[3]
    copy = pltpu.make_async_copy(records.at[t], heard, sem)
    copy.start()
    places = receiver_pos[...]
    for r in range(0, receivers, LANES):
        column = as_column(places[:, r : r + LANES].astype(jnp.float32)).astype(jnp.int32)
        hits[r : r + LANES, :] = jnp.where(iota((LANES, width), 1) == column, 1.0, 0.0).astype(jnp.bfloat16)
    copy.wait()
    pieces = jnp.concatenate([piece for c in range(2) for piece in pieces_of(heard[c], 3)], axis=0)
    for x in range(0, width, 512):
        found = jnp.dot(pieces, hits[:, x : x + 512], preferred_element_type=jnp.float32)
        for c in range(2):
            part = [found[(3 * c + i) * freqs : (3 * c + i + 1) * freqs] for i in range(3)]
            planes[c, :, x : x + 512] = part[0] + part[1] + part[2]


def surface_field(shape, t, f0, wavelet, source_pos, planes, flat, state):
    rows = shape.rows
    for c in range(4):
        if c < 2:
            strength = as_column(wavelet[t, c : c + 1, :])[f0 : f0 + rows]

            def natural(x, strength=strength):
                return jnp.where(iota((rows, LANES), 1) == source_pos[0] - x, strength, 0.0)
        else:
            def natural(x, c=c):
                return planes[c - 2, f0 : f0 + rows, x : x + LANES]
        load_field(shape, natural, c, flat, state)


class Work:
    def __init__(self, refs):
        self.state, self.totals, self.flat, self.known = refs[:4]
        self.products, self.weights, self.tables, self.gains = refs[4:6], refs[6:8], refs[8:10], refs[10:12]


def work_scratch(shape, models):
    cells = SUB * shape.steps
    square = pltpu.VMEM((cells, LANES), jnp.float32)
    return [
        pltpu.VMEM((4, cells, LANES), jnp.float32),
        square,
        square,
        pltpu.VMEM((cells, models * LANES), jnp.bfloat16),
        square,
        square,
        pltpu.VMEM((2 * LANES, 2 * LANES), jnp.bfloat16),
        pltpu.VMEM((2 * LANES, 2 * LANES), jnp.bfloat16),
        pltpu.VMEM((cells, 2 * LANES), jnp.float32),
        pltpu.VMEM((cells, 2 * LANES), jnp.float32),
        square,
        square,
    ]


def run_layers(shape, work, w_row, models, first=0, contribute=True):
    count = LAYERS * len(models)

    def look(i):
        t, l = i // LAYERS, i % LAYERS
        at = LAYERS * shape.parts + l
        known = work.known[:, (first + t) * LANES : (first + t + 1) * LANES]
        layer_tables(
            shape, l, w_row, models[t][at : at + 1, 0:LEVELS], known,
            work.weights[i % 2], work.tables[i % 2], work.gains[i % 2],
        )

    look(0)
    for i in range(count):
        if i + 1 < count:
            look(i + 1)
        layer_step(shape, work.state, work.tables[i % 2], work.gains[i % 2], work.products[i % 2])
        if contribute:
            add_contribution(shape, first * LAYERS + i, work.products[i % 2], work.totals)


def w_row_of(angular, f0, rows):
    return repeated(as_column(angular)[f0 : f0 + rows])


def start_all(copies):
    for copy in copies:
        copy.start()


def wait_all(copies):
    for copy in copies:
        copy.wait()


def begin_kernel(
    shape,
    table, index, records, receiver_pos, wavelet, source_pos,
    model, planes, top,
    own_table, own_index, places, heard, hits, found, own_wavelet, kept, sems,
):
    parts, cells = shape.parts, shape.cells
    copies = [
        pltpu.make_async_copy(table, own_table, sems.at[0]),
        pltpu.make_async_copy(index, own_index, sems.at[1]),
    ]
    start_all(copies)
    wait_all(copies)
    number = own_index[...].astype(jnp.float32)
    for l in range(LAYERS):
        for q in range(parts):
            model[l * parts + q : l * parts + q + 1, :] = number[l : l + 1, q * cells : (q + 1) * cells]
    model[LAYERS * parts : LAYERS * parts + LAYERS, 0:LEVELS] = own_table[...]
    d = lax.axis_index("depth")

    @pl.when(d < 2)
    def _():
        copies = [
            pltpu.make_async_copy(receiver_pos, places, sems.at[0]),
            pltpu.make_async_copy(wavelet, own_wavelet, sems.at[1]),
        ]
        start_all(copies)
        wait_all(copies)
        hear(jnp.where(d == 0, TICKS - 1, TICKS - 2), records, places, heard, hits, found, sems.at[0])

    @pl.when(d == 0)
    def _():
        for c in range(2):
            strength = as_column(own_wavelet[TICKS - 1, c : c + 1, :])
            kept[c] = jnp.where(iota(kept.shape[1:], 1) == source_pos[0], strength, 0.0)
            kept[2 + c] = found[c]
        copy = pltpu.make_async_copy(kept, top, sems.at[0])
        copy.start()
        copy.wait()

    @pl.when(d == 1)
    def _():
        copy = pltpu.make_async_copy(found, planes, sems.at[0])
        copy.start()
        copy.wait()


def own_layers(shape, chunks, fields, angular, model, held, own_angular, sems, work, each):
    rows = shape.rows
    angles = pltpu.make_async_copy(angular, own_angular, sems.at[chunks])
    copies = [pltpu.make_async_copy(fields.at[0, :, pl.ds(i * rows, rows), :], held.at[i], sems.at[i]) for i in range(chunks)]
    start_all([angles] + copies)
    load_known(shape, (model,), work.flat, work.known)
    work.totals[...] = jnp.zeros(work.totals.shape, jnp.float32)
    angles.wait()
    for i in range(chunks):
        copies[i].wait()
        for c in range(4):
            load_field(shape, lambda x, c=c: held[i, c, :, x : x + LANES], c, work.flat, work.state)
        w_row = w_row_of(own_angular[...], i * rows, rows)
        run_layers(shape, work, w_row, (model,))
        each(i, w_row)


def first_kernel(
    shape, chunks, devices,
    fields, angular, model, surface_angular, records, receiver_pos, wavelet, source_pos,
    after, image, w_rows,
    held, own_angular, own_surface, own_wavelet, places, heard, hits, found, sems, *scratch,
):
    work = Work(scratch)
    rows = shape.rows
    d = lax.axis_index("depth")

    def keep(i, w_row):
        after[i] = work.state[...]
        w_rows[i * SUB : (i + 1) * SUB, :] = jnp.broadcast_to(w_row, (SUB, LANES))

    @pl.when(d < devices - 1)
    def _():
        own_layers(shape, chunks, fields, angular, model, held, own_angular, sems, work, keep)
        image_of(shape, work.totals, image)

    @pl.when(d == devices - 1)
    def _():
        copies = [
            pltpu.make_async_copy(receiver_pos, places, sems.at[0]),
            pltpu.make_async_copy(surface_angular, own_surface, sems.at[1]),
            pltpu.make_async_copy(wavelet, own_wavelet, sems.at[2]),
        ]
        start_all(copies)
        wait_all(copies)
        hear(0, records, places, heard, hits, found, sems.at[0])
        for i in range(chunks):
            surface_field(shape, 0, i * rows, own_wavelet, source_pos, found, work.flat, work.state)
            keep(i, w_row_of(own_surface[0:1, :], i * rows, rows))
        image[...] = jnp.zeros(image.shape, jnp.float32)


def rows_at(ref, l, parts):
    return ref[l * parts : (l + 1) * parts, :]


def next_kernel(shape, freqs, devices, chunk, *refs):
    rows, parts = shape.rows, shape.parts
    after, w_rows, mate, two, mate_two, *refs = refs
    d = lax.axis_index("depth")
    if chunk:
        before, next_a, sent, own, next1, next2, up, shared, image, *scratch = refs
    else:
        sent, image, *scratch = refs
    work = Work(scratch)
    work.state[...] = after[chunk]
    models = (jnp.where(d % 2 == 0, mate[...], mate_two[...]), two)
    load_known(shape, models, work.flat, work.known)
    work.totals[...] = jnp.zeros(work.totals.shape, jnp.float32)
    run_layers(shape, work, w_rows[chunk * SUB : chunk * SUB + 1, :], models)
    for c in range(4):
        def put(x, value, c=c):
            sent[c * rows : (c + 1) * rows, x : x + LANES] = value
        store_field(shape, c, work.state, put)
    image_of(shape, work.totals, image)
    if not chunk:
        return
    scale = 1.0 / math.sqrt(freqs)
    count = LAYERS * TICKS
    found = []
    for l in range(count):
        if l < LAYERS:
            value = rows_at(before, l, parts) * scale
        else:
            value = (rows_at(image, l - LAYERS, parts) + rows_at(next_a, l - LAYERS, parts)) * scale
        if l >= 2 * LAYERS:
            value = jnp.where(d == devices - 2, 0.0, value)
        found.append(value)

    def beside(l, other):
        lower = max(l, other)
        return found[other] if lower % LAYERS else jnp.where(d == devices - lower // LAYERS, 0.0, found[other])

    def filtered(l):
        total = 2.0 * found[l]
        if l > 0:
            total = total - 0.5 * beside(l, l - 1)
        if l + 1 < count:
            total = total - 0.5 * beside(l, l + 1)
        return total

    up[...] = -0.5 * found[0]
    for t, out in enumerate((own, next1, next2)):
        for l in range(LAYERS):
            out[l * parts : (l + 1) * parts, :] = filtered(t * LAYERS + l)
    sent[4 * rows : 4 * rows + parts, 0 : shape.cells] = -0.5 * found[count - 1]
    near = LAYERS * parts
    even = d % 2 == 0
    shared[0:near, :] = jnp.where(even, next1[...], 0.0)
    shared[near : 2 * near, :] = jnp.where(even, next2[...], 0.0)

    @pl.when(jnp.logical_not(even))
    def _():
        shared[near - parts : near, :] = up[...]


def late_kernel(
    shape, chunks, devices,
    fields, angular, surface_angular, wavelet, source_pos, planes, model, mate, _,
    out, shared, extra,
    held, part, kept, image, own_angular, own_surface, own_wavelet, sems, *scratch,
):
    work = Work(scratch)
    rows, parts = shape.rows, shape.parts
    d = lax.axis_index("depth")
    shared[...] = jnp.zeros(shared.shape, jnp.float32)
    extra[...] = jnp.zeros(extra.shape, jnp.float32)

    def filtered():
        image_of(shape, work.totals, image)
        scale = 1.0 / math.sqrt(chunks * rows)
        found = [rows_at(image, l, parts) * scale for l in range(LAYERS)]
        totals = []
        for l in range(LAYERS):
            total = 2.0 * found[l]
            if l > 0:
                total = total - 0.5 * found[l - 1]
            if l + 1 < LAYERS:
                total = total - 0.5 * found[l + 1]
            totals.append(total)
        return found, totals

    @pl.when(d == 1)
    def _():
        copies = [
            pltpu.make_async_copy(planes, part, sems.at[0]),
            pltpu.make_async_copy(surface_angular, own_surface, sems.at[1]),
            pltpu.make_async_copy(wavelet, own_wavelet, sems.at[2]),
        ]
        start_all(copies)
        load_known(shape, (mate,), work.flat, work.known)
        work.totals[...] = jnp.zeros(work.totals.shape, jnp.float32)
        wait_all(copies)
        for i in range(chunks):
            surface_field(shape, 1, i * rows, own_wavelet, source_pos, part, work.flat, work.state)
            run_layers(shape, work, w_row_of(own_surface[1:2, :], i * rows, rows), (mate,))
            for c in range(4):
                def put(x, value, c=c):
                    kept[c, i * rows : (i + 1) * rows, x : x + LANES] = value
                store_field(shape, c, work.state, put)
        copy = pltpu.make_async_copy(kept, out, sems.at[0])
        copy.start()
        found, totals = filtered()
        for l in range(LAYERS):
            shared[l * parts : (l + 1) * parts, :] = totals[l]
        extra[0:parts, :] = -0.5 * found[LAYERS - 1]
        copy.wait()

    @pl.when(d == devices - 1)
    def _():
        own_layers(shape, chunks, fields, angular, model, held, own_angular, sems, work, lambda i, w_row: None)
        found, totals = filtered()
        for l in range(LAYERS):
            extra[l * parts : (l + 1) * parts, :] = totals[l]
        shared[(LAYERS - 1) * parts : LAYERS * parts, :] = -0.5 * found[0]


def mix_kernel(next1, next2, up, other, out):
    near, parts = next1.shape[0], up.shape[0]
    even = lax.axis_index("depth") % 2 == 0
    out[0:near, :] = jnp.where(even, 0.0, other[near : 2 * near, :] + next1[...])
    out[near : 2 * near, :] = jnp.where(even, 0.0, next2[...])

    @pl.when(even)
    def _():
        out[near - parts : near, :] = up[...]


def pass_kernel(crossed, late, out):
    near = late.shape[0]
    out[...] = jnp.where(lax.axis_index("depth") % 2 == 0, crossed[near : 2 * near, :], late[...])


def close_kernel(first, relayed, second, top, top1, own, other, crossed, passed, extra, section, fields_out, sems):
    near, cells = own.shape
    parts = near // LAYERS
    rows = relayed.shape[0] // 4
    d = lax.axis_index("depth")

    def moves(source, start, slot):
        return [
            pltpu.make_async_copy(
                source.at[pl.ds(c * rows, rows), :], fields_out.at[0, c, pl.ds(start, rows), :], sems.at[slot + c]
            )
            for c in range(4)
        ]

    for index, field in enumerate((top, top1)):
        @pl.when(d == index)
        def _(field=field):
            for c in range(4):
                for i in range(2):
                    at = pl.ds(i * rows, rows)
                    pltpu.make_async_copy(field.at[c, at, :], fields_out.at[0, c, at, :], sems.at[4 * i + c]).start()

    @pl.when(d > 1)
    def _():
        start_all(moves(second, rows, 4))

        @pl.when(d % 4 == 1)
        def _():
            start_all(moves(relayed, 0, 0))

        @pl.when(d % 4 != 1)
        def _():
            start_all(moves(first, 0, 0))

    total = own[...] + other[0:near, :] + crossed[0:near, :] + passed[...] + extra[...]
    for l in range(LAYERS):
        rows_of = total[l * parts : (l + 1) * parts, :]
        if l == 0:
            rows_of = rows_of + second[4 * rows : 4 * rows + parts, 0:cells]
        for q in range(parts):
            section[l : l + 1, q * cells : (q + 1) * cells] = rows_of[q : q + 1, :]
    wait_all(moves(first, 0, 0) + moves(second, rows, 4))


VMEM = pl.BlockSpec(memory_space=pltpu.VMEM)
SMEM = pl.BlockSpec(memory_space=pltpu.SMEM)
HBM = pl.BlockSpec(memory_space=pltpu.HBM)
ANY = pl.BlockSpec(memory_space=pl.ANY)
COST = pl.CostEstimate(flops=0, bytes_accessed=0, transcendentals=0)
PARAMS = pltpu.CompilerParams(vmem_limit_bytes=48 * 2**20)


def f32(*shape):
    return jax.ShapeDtypeStruct(shape, jnp.float32)


def on_device(
    devices,
    fields_in, flight_angular, wavelet, surface_angular, records, source_pos, receiver_pos, vel_table, vel_index,
):
    width = fields_in.shape[3]
    freqs = fields_in.shape[2]
    receivers = records.shape[3]
    rows = freqs // 2
    shape = Shape(rows, width)
    parts, cells = shape.parts, shape.cells
    axis = "depth"
    near, row = f32(LAYERS * parts, cells), f32(parts, cells)
    model_rows = LAYERS * parts + SUB
    chunk = f32(4 * rows + SUB, width)
    state = f32(4, SUB * shape.steps, LANES)
    planes_shape = f32(2, freqs, width)
    planes_scratch = pltpu.VMEM((2, freqs, width), jnp.float32)

    def image_scratch(ticks):
        return pltpu.VMEM((ticks * LAYERS * parts, cells), jnp.float32)

    def call(body, outs, ins, scratch, name):
        return pl.pallas_call(
            body,
            out_shape=[shape for shape, _ in outs],
            in_specs=[spec for _, spec in ins],
            out_specs=[spec for _, spec in outs],
            scratch_shapes=scratch,
            compiler_params=PARAMS,
            cost_estimate=COST,
            name=name,
        )(*[value if spec is not HBM else pltpu.with_memory_space_constraint(value, pltpu.HBM) for value, spec in ins])

    def swapped(value):
        return lax.ppermute(value, axis, [(i, i + 1 - 2 * (i % 2)) for i in range(devices)])

    chunks = 2
    last = devices - 1
    positions = receiver_pos.reshape(1, receivers)
    row_of = lambda value: pltpu.VMEM(value.shape, value.dtype)
    hearing = [
        row_of(positions), pltpu.VMEM((2, freqs, receivers), jnp.float32), pltpu.VMEM((receivers, width), jnp.bfloat16),
        planes_scratch,
    ]
    model, planes1, top = call(
        lambda *refs: begin_kernel(shape, *refs),
        [(f32(model_rows, cells), VMEM), (planes_shape, ANY), (f32(4, freqs, width), ANY)],
        [(vel_table, HBM), (vel_index, HBM), (records, HBM), (positions, HBM), (wavelet, HBM), (source_pos, SMEM)],
        [row_of(vel_table), row_of(vel_index)]
        + hearing
        + [row_of(wavelet), pltpu.VMEM((4, freqs, width), jnp.float32), pltpu.SemaphoreType.DMA((2,))],
        "begin",
    )
    mate = swapped(model)
    two = lax.ppermute(lax.optimization_barrier((model, mate))[0], axis, [(i, (i - 2) % devices) for i in range(devices)])
    held = pltpu.VMEM((chunks, 4, rows, width), jnp.float32)
    sems = pltpu.SemaphoreType.DMA((chunks + 1,))
    after, before, w_rows = call(
        lambda *refs: first_kernel(shape, chunks, devices, *refs),
        [
            (f32(chunks, 4, SUB * shape.steps, LANES), VMEM), (near, VMEM), (f32(chunks * SUB, LANES), VMEM),
        ],
        [
            (fields_in, HBM), (flight_angular, HBM), (model, VMEM), (surface_angular, HBM), (records, HBM), (positions, HBM),
            (wavelet, HBM), (source_pos, SMEM),
        ],
        [held, row_of(flight_angular), row_of(surface_angular), row_of(wavelet)] + hearing + [sems] + work_scratch(shape, 1),
        "first",
    )
    mate_two = swapped(lax.optimization_barrier((two, w_rows))[0])
    on = [(i, i + 3) for i in range(devices - 3)] + [(last, 2)]
    via = [(i, i - 1) if i % 4 == 2 else (i, j) for i, j in on]
    relay = [(i, i + 4) for i in range(1, devices - 4, 4)]
    common = [
        (after, VMEM), (w_rows, VMEM), (mate, VMEM), (two, VMEM), (mate_two, VMEM),
    ]
    again = work_scratch(shape, 2)
    both = f32(2 * LAYERS * parts, cells)
    sent1, next_a = call(
        lambda *refs: next_kernel(shape, freqs, devices, 0, *refs),
        [(f32(4 * rows, width), VMEM), (f32(2 * LAYERS * parts, cells), VMEM)],
        common,
        again,
        "next",
    )
    first = lax.ppermute(sent1, axis, via)
    sent2, own, next1, next2, up, shared = call(
        lambda *refs: next_kernel(shape, freqs, devices, 1, *refs),
        [(chunk, VMEM), (near, VMEM), (near, VMEM), (near, VMEM), (row, VMEM), (both, VMEM)],
        common + [(before, VMEM), (next_a, VMEM)],
        [image_scratch(2)] + again,
        "next",
    )
    second = lax.ppermute(sent2, axis, on)
    other = swapped(shared)
    (mixed,) = call(mix_kernel, [(both, VMEM)], [(next1, VMEM), (next2, VMEM), (up, VMEM), (other, VMEM)], [], "mix")
    crossed = lax.ppermute(
        mixed, axis, [(i, (i + 1) % devices) for i in range(1, devices, 2)] + [(i, i - 1) for i in range(2, devices, 2)]
    )
    relayed = lax.ppermute(lax.optimization_barrier((first, mixed))[0], axis, relay)
    top1, late, extra = call(
        lambda *refs: late_kernel(shape, chunks, devices, *refs),
        [(f32(4, freqs, width), ANY), (near, VMEM), (near, VMEM)],
        [
            (fields_in, HBM), (flight_angular, HBM), (surface_angular, HBM), (wavelet, HBM), (source_pos, SMEM),
            (planes1, ANY), (model, VMEM), (mate, VMEM), (mixed, VMEM),
        ],
        [
            held, planes_scratch, pltpu.VMEM((4, freqs, width), jnp.float32), image_scratch(1),
            row_of(flight_angular), row_of(surface_angular), row_of(wavelet), sems,
        ]
        + work_scratch(shape, 1),
        "late",
    )
    (passing,) = call(pass_kernel, [(near, VMEM)], [(crossed, VMEM), (late, VMEM)], [], "pass")
    passed = swapped(passing)
    section, fields_out = call(
        close_kernel,
        [(f32(LAYERS, width), VMEM), (f32(1, 4, freqs, width), ANY)],
        [
            (first, VMEM), (relayed, VMEM), (second, VMEM), (top, ANY), (top1, ANY),
            (own, VMEM), (other, VMEM), (crossed, VMEM), (passed, VMEM), (extra, VMEM),
        ],
        [pltpu.SemaphoreType.DMA((8,))],
        "close",
    )
    return section, fields_out


def solution(mesh):
    placed = (
        P("depth", None, "shots", None),
        P("depth", "shots"),
        P(None, None, "shots"),
        P(None, "shots"),
        P(None, None, "shots", None),
        P("shots"),
        P("shots"),
        P("depth", None),
        P("depth", None),
    )
    devices = mesh.shape["depth"]

    def run(*args):
        return on_device(devices, *args)

    return jax.shard_map(
        run,
        mesh=mesh,
        in_specs=placed,
        out_specs=(P("depth", "shots"), P("depth", None, "shots", None)),
        check_vma=False,
    )
```

time: 53.5 us -> 45.8 us (0.86)
  the two profiles are of different devices: /device:TPU:1 before, /device:TPU:9 now
where the time goes in v2:
time: 45.8 us; the launch traced here: 45.5 us
  starting transfers between devices  21.9 us (48%)
  Pallas kernels  15.3 us (33%)
  waiting for transfers between devices  6.7 us (15%)
  between operations  1.57 us (3%)
    pallas_call x8, Pallas kernels, call(): pl.pallas_call(body, out_shape=[shape for shape, _ in outs], in_specs=[sp...  15.3 us
    ppermute x4, starting transfers between devices, swapped(): lax.ppermute(value, axis, [(i, i + 1 - 2 * (i % 2)) for i in range(device...  8.97 us
    ppermute x1, waiting for transfers between devices, on_device(): lax.ppermute(mixed, axis, [(i, (i + 1) % devices) for i in range(1, devic...  4.08 us
    ppermute x1, starting transfers between devices, on_device(): second = lax.ppermute(sent2, axis, on)  3.57 us
    ppermute x1, starting transfers between devices, on_device(): first = lax.ppermute(sent1, axis, via)  3.44 us
    ppermute x1, starting transfers between devices, on_device(): lax.ppermute(lax.optimization_barrier((first, mixed))[0], axis, relay)  2.9 us
    ppermute x4, waiting for transfers between devices, swapped(): lax.ppermute(value, axis, [(i, i + 1 - 2 * (i % 2)) for i in range(device...  2.6 us
    ppermute x1, starting transfers between devices, on_device(): lax.ppermute(mixed, axis, [(i, (i + 1) % devices) for i in range(1, devic...  1.92 us
  transfers between devices with their start and end apart: 9, of which 4 were waited for; matrix products, arithmetic and copies ran while one was open for 0% of the time, Pallas kernels for 20%

profile of v2, /device:TPU:9, one launch (start us, length us, event | category | flops | bytes accessed | tf_op | source)
XLA Modules:
  0.0 45.5 jit_solution(12432127238219730904)
XLA Ops:
  1.3 0.8 %begin.1 = (f32[40,256]{1,0:T(8,128)S(1)}, f32[2,32,2048]{2,1,0:T(8,128)S(1)}, f32[4,32,2048]{2,1,0:T(8,128)S(1)}) custom-call(f32[4,16]{1,0:T(4,128)} %refs_0_.3, s32[4,2048]{1,0:T(4,128)} %refs_1_.3, f32[3,2,32,1024]{3,2,1,0:T(8,128)} %refs_4_.4, s32[1,1024]{1,0:T(1,128)} %bitcast.1, f32[3,2,32]{2,1,0:T(2,128)} %refs_3_.3, s32[1]{0:T(128)S(6)} %copy.11.refs_5_.refs_7_.refs_4_), custom_call_target="tpu_custom_call" | custom-call | tf_op jit(solution)/shard_map/begin/pallas_call | solution.py:613
  2.1 0.7 %collective-permute-start = (f32[40,256]{1,0:T(8,128)S(1)}, f32[40,256]{1,0:T(8,128)S(1)}, u32[]{:S(2)}, u32[]{:S(2)}) collective-permute-start(f32[40,256]{1,0:T(8,128)S(1)} %get-tuple-element.25.refs_2_.refs_6_), channel_id=1, source_target_pairs={{0,1},{1,0},{2,3},{3,2},{4,5},{5,4},{6,7},{7,6},{8,9},{9,8},{10,11... | collective-permute-start | bytes 122888 | tf_op jit(solution)/shard_map/ppermute | solution.py:625
  2.8 0.9 %collective-permute-done.refs_2_.refs_7_ = f32[40,256]{1,0:T(8,128)S(1)} collective-permute-done((f32[40,256]{1,0:T(8,128)S(1)}, f32[40,256]{1,0:T(8,128)S(1)}, u32[]{:S(2)}, u32[]{:S(2)}) %collective-permute-start) | collective-permute-done | bytes 40992 | tf_op jit(solution)/shard_map/ppermute | solution.py:625
  3.7 1.1 %collective-permute-start.1 = (f32[40,256]{1,0:T(8,128)S(1)}, f32[40,256]{1,0:T(8,128)S(1)}, u32[]{:S(2)}, u32[]{:S(2)}) collective-permute-start(f32[40,256]{1,0:T(8,128)S(1)} %get-tuple-element.25.refs_2_.refs_6_), channel_id=1, source_target_pairs={{0,14},{1,15},{2,0},{3,1},{4,2},{5,3},{6,4},{7,5},{8,6},{9,7},{10,... | collective-permute-start | bytes 122888 | tf_op jit(solution)/shard_map/ppermute | solution.py:645
  4.8 5.3 %first.1 = (f32[2,4,256,128]{3,2,1,0:T(8,128)S(1)}, f32[32,256]{1,0:T(8,128)S(1)}, f32[16,128]{1,0:T(8,128)S(1)}) custom-call(f32[1,4,32,2048]{3,2,1,0:T(8,128)} %refs_0_.5, f32[1,32]{1,0:T(1,128)} %refs_1_.5, f32[40,256]{1,0:T(8,128)S(1)} %get-tuple-element.25.refs_2_.refs_6_, f32[3,32]{1,0:T(4,128)} %refs_2_.3, f32[3,2,32,1024]{3,2,1,0:T(8,128)} %refs_4_.4, ...), custom_call_target="tpu_custom_call" | custom-call | tf_op jit(solution)/shard_map/first/pallas_call | solution.py:613
  10.1 0.0 collective-permute-done.1.refs_3_
  10.1 0.7 %collective-permute-start.2 = (f32[40,256]{1,0:T(8,128)S(1)}, f32[40,256]{1,0:T(8,128)S(1)}, u32[]{:S(2)}, u32[]{:S(2)}) collective-permute-start(f32[40,256]{1,0:T(8,128)S(1)} %collective-permute-done.1.refs_3_), channel_id=1, source_target_pairs={{0,1},{1,0},{2,3},{3,2},{4,5},{5,4},{6,7},{7,6},{8,9},{9,8},{10,11... | collective-permute-start | bytes 122888 | tf_op jit(solution)/shard_map/ppermute | solution.py:625
  10.8 0.9 %collective-permute-done.2.refs_4_ = f32[40,256]{1,0:T(8,128)S(1)} collective-permute-done((f32[40,256]{1,0:T(8,128)S(1)}, f32[40,256]{1,0:T(8,128)S(1)}, u32[]{:S(2)}, u32[]{:S(2)}) %collective-permute-start.2) | collective-permute-done | bytes 40992 | tf_op jit(solution)/shard_map/ppermute | solution.py:625
  11.7 3.6 %next.2 = (f32[64,2048]{1,0:T(8,128)S(1)}, f32[64,256]{1,0:T(8,128)S(1)}) custom-call(f32[2,4,256,128]{3,2,1,0:T(8,128)S(1)} %get-tuple-element.23.refs_0_, f32[16,128]{1,0:T(8,128)S(1)} %get-tuple-element.24.refs_1_, f32[40,256]{1,0:T(8,128)S(1)} %collective-permute-done.refs_2_.refs_7_, f32[40,256]{1,0:T(8,128)S(1)} %collective-permute-done.1.refs_3_, ...), custom_call_target="tpu_custom_call" | custom-call | tf_op jit(solution)/shard_map/next/pallas_call | solution.py:613
  15.3 3.4 %collective-permute-start.3 = (f32[64,2048]{1,0:T(8,128)S(1)}, f32[64,2048]{1,0:T(8,128)S(1)}, u32[]{:S(2)}, u32[]{:S(2)}) collective-permute-start(f32[64,2048]{1,0:T(8,128)S(1)} %get-tuple-element.27), channel_id=1, source_target_pairs={{0,3},{1,4},{2,1},{3,6},{4,7},{5,8},{6,5},{7,10},{8,11},{9,12},{10... | collective-permute-start | bytes 1572872 | tf_op jit(solution)/shard_map/ppermute | solution.py:676
  18.8 3.6 %next.3 = (f32[72,2048]{1,0:T(8,128)S(1)}, f32[32,256]{1,0:T(8,128)S(1)}, f32[32,256]{1,0:T(8,128)S(1)}, f32[32,256]{1,0:T(8,128)S(1)}, f32[8,256]{1,0:T(8,128)S(1)}, /*index=5*/f32[64,256]{1,0:T(8,128)S(1)}) custom-call(f32[2,4,256,128]{3,2,1,0:T(8,128)S(1)} %get-tuple-element.23.refs_0_, f32[16,128]{1,0:T(8,128)S(1)} %get-tuple-element.24.refs_1_, ...), custom_call_target="tpu_custom_call" | custom-call | tf_op jit(solution)/shard_map/next/pallas_call | solution.py:613
  22.4 0.1 collective-permute-start.4
  22.5 3.6 %collective-permute-start.6 = (f32[72,2048]{1,0:T(8,128)S(1)}, f32[72,2048]{1,0:T(8,128)S(1)}, u32[]{:S(2)}, u32[]{:S(2)}) collective-permute-start(f32[72,2048]{1,0:T(8,128)S(1)} %get-tuple-element.35), channel_id=1, source_target_pairs={{0,3},{1,4},{2,5},{3,6},{4,7},{5,8},{6,9},{7,10},{8,11},{9,12},{10... | collective-permute-start | bytes 1769480 | tf_op jit(solution)/shard_map/ppermute | solution.py:684
  26.1 0.0 collective-permute-done.4.other
  26.1 0.0 collective-permute-done.3.first
  26.1 2.9 %collective-permute-start.5 = (f32[64,2048]{1,0:T(8,128)S(1)}, f32[64,2048]{1,0:T(8,128)S(1)}, u32[]{:S(2)}, u32[]{:S(2)}) collective-permute-start(f32[64,2048]{1,0:T(8,128)S(1)} %collective-permute-done.3.first), channel_id=1, source_target_pairs={{1,5},{5,9},{9,13},{17,21},{21,25},{25,29}} | collective-permute-start | bytes 1572872 | tf_op jit(solution)/shard_map/ppermute | solution.py:690
  29.0 1.9 %collective-permute-start.7 = (f32[64,256]{1,0:T(8,128)S(1)}, f32[64,256]{1,0:T(8,128)S(1)}, u32[]{:S(2)}, u32[]{:S(2)}) collective-permute-start(f32[64,256]{1,0:T(8,128)S(1)} %mix.1.refs_8_), channel_id=1, source_target_pairs={{1,2},{3,4},{5,6},{7,8},{9,10},{11,12},{13,14},{15,0},{2,1},{4,3},... | collective-permute-start | bytes 196616 | tf_op jit(solution)/shard_map/ppermute | solution.py:687
  30.9 0.3 late.1
  31.2 4.1 %collective-permute-done.7.crossed = f32[64,256]{1,0:T(8,128)S(1)} collective-permute-done((f32[64,256]{1,0:T(8,128)S(1)}, f32[64,256]{1,0:T(8,128)S(1)}, u32[]{:S(2)}, u32[]{:S(2)}) %collective-permute-start.7) | collective-permute-done | bytes 65568 | tf_op jit(solution)/shard_map/ppermute | solution.py:687
  35.3 7.5 %collective-permute-start.8 = (f32[32,256]{1,0:T(8,128)S(1)}, f32[32,256]{1,0:T(8,128)S(1)}, u32[]{:S(2)}, u32[]{:S(2)}) collective-permute-start(f32[32,256]{1,0:T(8,128)S(1)} %pass.1), channel_id=1, source_target_pairs={{0,1},{1,0},{2,3},{3,2},{4,5},{5,4},{6,7},{7,6},{8,9},{9,8},{10,11... | collective-permute-start | bytes 98312 | tf_op jit(solution)/shard_map/ppermute | solution.py:625
  42.8 0.9 %collective-permute-done.8.passed = f32[32,256]{1,0:T(8,128)S(1)} collective-permute-done((f32[32,256]{1,0:T(8,128)S(1)}, f32[32,256]{1,0:T(8,128)S(1)}, u32[]{:S(2)}, u32[]{:S(2)}) %collective-permute-start.8) | collective-permute-done | bytes 32800 | tf_op jit(solution)/shard_map/ppermute | solution.py:625
  43.6 0.0 collective-permute-done.6.second
  43.6 0.0 collective-permute-done.5.relayed
  43.7 1.7 %close.1 = (f32[4,2048]{1,0:T(4,128)}, f32[1,4,32,2048]{3,2,1,0:T(8,128)}) custom-call(f32[64,2048]{1,0:T(8,128)S(1)} %collective-permute-done.3.first, f32[64,2048]{1,0:T(8,128)S(1)} %collective-permute-done.5.relayed, f32[72,2048]{1,0:T(8,128)S(1)} %collective-permute-done.6.second, f32[4,32,2048]{2,1,0:T(8,128)S(1)} %get-tuple-element.36.top, ...), custom_call_target="tpu_custom_call" | custom-call | tf_op jit(solution)/shard_map/close/pallas_call | solution.py:613
  (2 shorter events, 0.0 us)
Async XLA Ops:
  2.1 1.6 %collective-permute-start = (f32[40,256]{1,0:T(8,128)S(1)}, f32[40,256]{1,0:T(8,128)S(1)}, u32[]{:S(2)}, u32[]{:S(2)}) collective-permute-start(f32[40,256]{1,0:T(8,128)S(1)} %get-tuple-element.25.refs_2_.refs_6_), channel_id=1, source_target_pairs={{0,1},{1,0},{2,3},{3,2},{4,5},{5,4},{6,7},{7,6},{8,9},{9,8},{10,11... | collective-permute-start | bytes 122888 | tf_op jit(solution)/shard_map/ppermute | solution.py:625
  3.7 6.4 %collective-permute-start.1 = (f32[40,256]{1,0:T(8,128)S(1)}, f32[40,256]{1,0:T(8,128)S(1)}, u32[]{:S(2)}, u32[]{:S(2)}) collective-permute-start(f32[40,256]{1,0:T(8,128)S(1)} %get-tuple-element.25.refs_2_.refs_6_), channel_id=1, source_target_pairs={{0,14},{1,15},{2,0},{3,1},{4,2},{5,3},{6,4},{7,5},{8,6},{9,7},{10,... | collective-permute-start | bytes 122888 | tf_op jit(solution)/shard_map/ppermute | solution.py:645
  10.1 1.6 %collective-permute-start.2 = (f32[40,256]{1,0:T(8,128)S(1)}, f32[40,256]{1,0:T(8,128)S(1)}, u32[]{:S(2)}, u32[]{:S(2)}) collective-permute-start(f32[40,256]{1,0:T(8,128)S(1)} %collective-permute-done.1.refs_3_), channel_id=1, source_target_pairs={{0,1},{1,0},{2,3},{3,2},{4,5},{5,4},{6,7},{7,6},{8,9},{9,8},{10,11... | collective-permute-start | bytes 122888 | tf_op jit(solution)/shard_map/ppermute | solution.py:625
  15.3 10.8 %collective-permute-start.3 = (f32[64,2048]{1,0:T(8,128)S(1)}, f32[64,2048]{1,0:T(8,128)S(1)}, u32[]{:S(2)}, u32[]{:S(2)}) collective-permute-start(f32[64,2048]{1,0:T(8,128)S(1)} %get-tuple-element.27), channel_id=1, source_target_pairs={{0,3},{1,4},{2,1},{3,6},{4,7},{5,8},{6,5},{7,10},{8,11},{9,12},{10... | collective-permute-start | bytes 1572872 | tf_op jit(solution)/shard_map/ppermute | solution.py:676
  22.4 3.7 %collective-permute-start.4 = (f32[64,256]{1,0:T(8,128)S(1)}, f32[64,256]{1,0:T(8,128)S(1)}, u32[]{:S(2)}, u32[]{:S(2)}) collective-permute-start(f32[64,256]{1,0:T(8,128)S(1)} %get-tuple-element.33), channel_id=1, source_target_pairs={{0,1},{1,0},{2,3},{3,2},{4,5},{5,4},{6,7},{7,6},{8,9},{9,8},{10,11... | collective-permute-start | bytes 196616 | tf_op jit(solution)/shard_map/ppermute | solution.py:625
  22.5 21.2 %collective-permute-start.6 = (f32[72,2048]{1,0:T(8,128)S(1)}, f32[72,2048]{1,0:T(8,128)S(1)}, u32[]{:S(2)}, u32[]{:S(2)}) collective-permute-start(f32[72,2048]{1,0:T(8,128)S(1)} %get-tuple-element.35), channel_id=1, source_target_pairs={{0,3},{1,4},{2,5},{3,6},{4,7},{5,8},{6,9},{7,10},{8,11},{9,12},{10... | collective-permute-start | bytes 1769480 | tf_op jit(solution)/shard_map/ppermute | solution.py:684
  26.1 17.5 %collective-permute-start.5 = (f32[64,2048]{1,0:T(8,128)S(1)}, f32[64,2048]{1,0:T(8,128)S(1)}, u32[]{:S(2)}, u32[]{:S(2)}) collective-permute-start(f32[64,2048]{1,0:T(8,128)S(1)} %collective-permute-done.3.first), channel_id=1, source_target_pairs={{1,5},{5,9},{9,13},{17,21},{21,25},{25,29}} | collective-permute-start | bytes 1572872 | tf_op jit(solution)/shard_map/ppermute | solution.py:690
  29.0 6.3 %collective-permute-start.7 = (f32[64,256]{1,0:T(8,128)S(1)}, f32[64,256]{1,0:T(8,128)S(1)}, u32[]{:S(2)}, u32[]{:S(2)}) collective-permute-start(f32[64,256]{1,0:T(8,128)S(1)} %mix.1.refs_8_), channel_id=1, source_target_pairs={{1,2},{3,4},{5,6},{7,8},{9,10},{11,12},{13,14},{15,0},{2,1},{4,3},... | collective-permute-start | bytes 196616 | tf_op jit(solution)/shard_map/ppermute | solution.py:687
  35.3 8.3 %collective-permute-start.8 = (f32[32,256]{1,0:T(8,128)S(1)}, f32[32,256]{1,0:T(8,128)S(1)}, u32[]{:S(2)}, u32[]{:S(2)}) collective-permute-start(f32[32,256]{1,0:T(8,128)S(1)} %pass.1), channel_id=1, source_target_pairs={{0,1},{1,0},{2,3},{3,2},{4,5},{5,4},{6,7},{7,6},{8,9},{9,8},{10,11... | collective-permute-start | bytes 98312 | tf_op jit(solution)/shard_map/ppermute | solution.py:625

commit v3 on v2

--- a/solution.py
+++ b/solution.py
@@ -332,22 +332,24 @@
         copy.start()
         copy.wait()
 
-    @pl.when(d == 1)
+        hear(1, records, places, heard, hits, found, sems.at[0])
+
+    @pl.when(d < 2)
     def _():
         copy = pltpu.make_async_copy(found, planes, sems.at[0])
         copy.start()
         copy.wait()
 
 
-def own_layers(shape, chunks, fields, angular, model, held, own_angular, sems, work, each):
+def own_layers(shape, which, fields, angular, model, held, own_angular, sems, work, each):
     rows = shape.rows
-    angles = pltpu.make_async_copy(angular, own_angular, sems.at[chunks])
-    copies = [pltpu.make_async_copy(fields.at[0, :, pl.ds(i * rows, rows), :], held.at[i], sems.at[i]) for i in range(chunks)]
-    start_all([angles] + copies)
+    angles = pltpu.make_async_copy(angular, own_angular, sems.at[sems.shape[0] - 1])
+    copies = {i: pltpu.make_async_copy(fields.at[0, :, pl.ds(i * rows, rows), :], held.at[i], sems.at[i]) for i in which}
+    start_all([angles] + list(copies.values()))
     load_known(shape, (model,), work.flat, work.known)
     work.totals[...] = jnp.zeros(work.totals.shape, jnp.float32)
     angles.wait()
-    for i in range(chunks):
+    for i in which:
         copies[i].wait()
         for c in range(4):
             load_field(shape, lambda x, c=c: held[i, c, :, x : x + LANES], c, work.flat, work.state)
@@ -359,7 +361,7 @@
 def first_kernel(
     shape, chunks, devices,
     fields, angular, model, surface_angular, records, receiver_pos, wavelet, source_pos,
-    after, image, w_rows,
+    after, image, w_rows, early,
     held, own_angular, own_surface, own_wavelet, places, heard, hits, found, sems, *scratch,
 ):
     work = Work(scratch)
@@ -372,7 +374,7 @@
 
     @pl.when(d < devices - 1)
     def _():
-        own_layers(shape, chunks, fields, angular, model, held, own_angular, sems, work, keep)
+        own_layers(shape, range(chunks), fields, angular, model, held, own_angular, sems, work, keep)
         image_of(shape, work.totals, image)
 
     @pl.when(d == devices - 1)
@@ -389,6 +391,8 @@
             surface_field(shape, 0, i * rows, own_wavelet, source_pos, found, work.flat, work.state)
             keep(i, w_row_of(own_surface[0:1, :], i * rows, rows))
         image[...] = jnp.zeros(image.shape, jnp.float32)
+        own_layers(shape, range(1), fields, angular, model, held, own_angular, sems, work, lambda i, w_row: None)
+        image_of(shape, work.totals, early)
 
 
 def rows_at(ref, l, parts):
@@ -400,7 +404,7 @@
     after, w_rows, mate, two, mate_two, *refs = refs
     d = lax.axis_index("depth")
     if chunk:
-        before, next_a, sent, own, next1, next2, up, shared, image, *scratch = refs
+        before, next_a, sent, own, shared, across, next2, image, *scratch = refs
     else:
         sent, image, *scratch = refs
     work = Work(scratch)
@@ -440,26 +444,23 @@
             total = total - 0.5 * beside(l, l + 1)
         return total
 
-    up[...] = -0.5 * found[0]
-    for t, out in enumerate((own, next1, next2)):
-        for l in range(LAYERS):
-            out[l * parts : (l + 1) * parts, :] = filtered(t * LAYERS + l)
+    even = d % 2 == 0
+    for l in range(LAYERS):
+        at = pl.ds(l * parts, parts)
+        own[at, :] = filtered(l)
+        below = filtered(LAYERS + l)
+        above = -0.5 * found[0] if l == LAYERS - 1 else jnp.zeros_like(below)
+        shared[at, :] = jnp.where(even, below, above)
+        across[at, :] = jnp.where(even, above, below)
+        next2[at, :] = filtered(2 * LAYERS + l)
     sent[4 * rows : 4 * rows + parts, 0 : shape.cells] = -0.5 * found[count - 1]
-    near = LAYERS * parts
-    even = d % 2 == 0
-    shared[0:near, :] = jnp.where(even, next1[...], 0.0)
-    shared[near : 2 * near, :] = jnp.where(even, next2[...], 0.0)
-
-    @pl.when(jnp.logical_not(even))
-    def _():
-        shared[near - parts : near, :] = up[...]
 
 
 def late_kernel(
     shape, chunks, devices,
-    fields, angular, surface_angular, wavelet, source_pos, planes, model, mate, _,
-    out, shared, extra,
-    held, part, kept, image, own_angular, own_surface, own_wavelet, sems, *scratch,
+    fields, angular, surface_angular, wavelet, source_pos, planes, model, mate, early, _,
+    out, out_more, shared, extra,
+    held, part, image, own_angular, own_surface, own_wavelet, sems, *scratch,
 ):
     work = Work(scratch)
     rows, parts = shape.rows, shape.parts
@@ -467,10 +468,12 @@
     shared[...] = jnp.zeros(shared.shape, jnp.float32)
     extra[...] = jnp.zeros(extra.shape, jnp.float32)
 
-    def filtered():
+    def filtered(more=None):
         image_of(shape, work.totals, image)
         scale = 1.0 / math.sqrt(chunks * rows)
         found = [rows_at(image, l, parts) * scale for l in range(LAYERS)]
+        if more is not None:
+            found = [value + rows_at(more, l, parts) * scale for l, value in enumerate(found)]
         totals = []
         for l in range(LAYERS):
             total = 2.0 * found[l]
@@ -481,7 +484,7 @@
             totals.append(total)
         return found, totals
 
-    @pl.when(d == 1)
+    @pl.when(d < 2)
     def _():
         copies = [
             pltpu.make_async_copy(planes, part, sems.at[0]),
@@ -489,91 +492,106 @@
             pltpu.make_async_copy(wavelet, own_wavelet, sems.at[2]),
         ]
         start_all(copies)
-        load_known(shape, (mate,), work.flat, work.known)
+        top_model = jnp.where(d == 0, model[...], mate[...])
+        load_known(shape, (top_model,), work.flat, work.known)
         work.totals[...] = jnp.zeros(work.totals.shape, jnp.float32)
         wait_all(copies)
         for i in range(chunks):
-            surface_field(shape, 1, i * rows, own_wavelet, source_pos, part, work.flat, work.state)
-            run_layers(shape, work, w_row_of(own_surface[1:2, :], i * rows, rows), (mate,))
-            for c in range(4):
-                def put(x, value, c=c):
-                    kept[c, i * rows : (i + 1) * rows, x : x + LANES] = value
-                store_field(shape, c, work.state, put)
-        copy = pltpu.make_async_copy(kept, out, sems.at[0])
-        copy.start()
+            @pl.when(d == 1 - i)
+            def _(i=i):
+                surface_field(shape, 1, i * rows, own_wavelet, source_pos, part, work.flat, work.state)
+        w_both = [w_row_of(own_surface[1:2, :], i * rows, rows) for i in range(chunks)]
+        run_layers(shape, work, jnp.where(d == 1, w_both[0], w_both[1]), (top_model,))
+        for c in range(4):
+            def put(x, value, c=c):
+                out[c * rows : (c + 1) * rows, x : x + LANES] = value
+                out_more[c * rows : (c + 1) * rows, x : x + LANES] = value
+            store_field(shape, c, work.state, put)
         found, totals = filtered()
-        for l in range(LAYERS):
-            shared[l * parts : (l + 1) * parts, :] = totals[l]
-        extra[0:parts, :] = -0.5 * found[LAYERS - 1]
-        copy.wait()
+
+        @pl.when(d == 1)
+        def _():
+            for l in range(LAYERS):
+                shared[l * parts : (l + 1) * parts, :] = totals[l]
+            extra[0:parts, :] = -0.5 * found[LAYERS - 1]
+
+        @pl.when(d == 0)
+        def _():
+            for l in range(LAYERS):
+                extra[l * parts : (l + 1) * parts, :] = totals[l]
+            shared[0:parts, :] = -0.5 * found[LAYERS - 1]
 
     @pl.when(d == devices - 1)
     def _():
-        own_layers(shape, chunks, fields, angular, model, held, own_angular, sems, work, lambda i, w_row: None)
-        found, totals = filtered()
+        own_layers(shape, range(1, chunks), fields, angular, model, held, own_angular, sems, work, lambda i, w_row: None)
+        found, totals = filtered(early)
         for l in range(LAYERS):
             extra[l * parts : (l + 1) * parts, :] = totals[l]
         shared[(LAYERS - 1) * parts : LAYERS * parts, :] = -0.5 * found[0]
 
 
-def mix_kernel(next1, next2, up, other, out):
-    near, parts = next1.shape[0], up.shape[0]
-    even = lax.axis_index("depth") % 2 == 0
-    out[0:near, :] = jnp.where(even, 0.0, other[near : 2 * near, :] + next1[...])
-    out[near : 2 * near, :] = jnp.where(even, 0.0, next2[...])
-
-    @pl.when(even)
-    def _():
-        out[near - parts : near, :] = up[...]
-
-
-def pass_kernel(crossed, late, out):
-    near = late.shape[0]
-    out[...] = jnp.where(lax.axis_index("depth") % 2 == 0, crossed[near : 2 * near, :], late[...])
-
-
-def close_kernel(first, relayed, second, top, top1, own, other, crossed, passed, extra, section, fields_out, sems):
-    near, cells = own.shape
-    parts = near // LAYERS
-    rows = relayed.shape[0] // 4
+def started(copies):
+    for copy in copies:
+        copy.start()
+    return copies
+
+
+def place_kernel(first, relayed, top, top1, more, fields_out, sems):
     d = lax.axis_index("depth")
-
-    def moves(source, start, slot):
+    rows = first.shape[0] // 4
+
+    def moves(source, start=0):
         return [
             pltpu.make_async_copy(
-                source.at[pl.ds(c * rows, rows), :], fields_out.at[0, c, pl.ds(start, rows), :], sems.at[slot + c]
+                source.at[pl.ds(c * rows, rows), :], fields_out.at[0, c, pl.ds(start, rows), :], sems.at[c + (4 if start else 0)]
             )
             for c in range(4)
         ]
 
-    for index, field in enumerate((top, top1)):
-        @pl.when(d == index)
-        def _(field=field):
-            for c in range(4):
-                for i in range(2):
-                    at = pl.ds(i * rows, rows)
-                    pltpu.make_async_copy(field.at[c, at, :], fields_out.at[0, c, at, :], sems.at[4 * i + c]).start()
+    @pl.when(d == 0)
+    def _():
+        wait_all(started([pltpu.make_async_copy(top, fields_out.at[0], sems.at[0])]))
+
+    @pl.when(d == 1)
+    def _():
+        wait_all(started(moves(top1) + moves(more, rows)))
+
+    @pl.when(jnp.logical_and(d > 1, d % 4 == 1))
+    def _():
+        wait_all(started(moves(relayed)))
+
+    @pl.when(jnp.logical_and(d > 1, d % 4 != 1))
+    def _():
+        wait_all(started(moves(first)))
+
+
+def close_kernel(placed, second, own, other, crossed, from2, late, extra, section, fields_out, sems):
+    near, cells = own.shape
+    parts = near // LAYERS
+    rows = (second.shape[0] - parts) // 4
+    d = lax.axis_index("depth")
+
+    def moves():
+        return [
+            pltpu.make_async_copy(second.at[pl.ds(c * rows, rows), :], fields_out.at[0, c, pl.ds(rows, rows), :], sems.at[c])
+            for c in range(4)
+        ]
 
     @pl.when(d > 1)
     def _():
-        start_all(moves(second, rows, 4))
-
-        @pl.when(d % 4 == 1)
-        def _():
-            start_all(moves(relayed, 0, 0))
-
-        @pl.when(d % 4 != 1)
-        def _():
-            start_all(moves(first, 0, 0))
-
-    total = own[...] + other[0:near, :] + crossed[0:near, :] + passed[...] + extra[...]
+        started(moves())
+
+    total = own[...] + other[...] + crossed[...] + from2[...] + late[...] + extra[...]
     for l in range(LAYERS):
         rows_of = total[l * parts : (l + 1) * parts, :]
         if l == 0:
             rows_of = rows_of + second[4 * rows : 4 * rows + parts, 0:cells]
         for q in range(parts):
             section[l : l + 1, q * cells : (q + 1) * cells] = rows_of[q : q + 1, :]
-    wait_all(moves(first, 0, 0) + moves(second, rows, 4))
+
+    @pl.when(d > 1)
+    def _():
+        wait_all(moves())
 
 
 VMEM = pl.BlockSpec(memory_space=pltpu.VMEM)
@@ -609,13 +627,14 @@
     def image_scratch(ticks):
         return pltpu.VMEM((ticks * LAYERS * parts, cells), jnp.float32)
 
-    def call(body, outs, ins, scratch, name):
+    def call(body, outs, ins, scratch, name, aliases={}):
         return pl.pallas_call(
             body,
             out_shape=[shape for shape, _ in outs],
             in_specs=[spec for _, spec in ins],
             out_specs=[spec for _, spec in outs],
             scratch_shapes=scratch,
+            input_output_aliases=aliases,
             compiler_params=PARAMS,
             cost_estimate=COST,
             name=name,
@@ -645,10 +664,11 @@
     two = lax.ppermute(lax.optimization_barrier((model, mate))[0], axis, [(i, (i - 2) % devices) for i in range(devices)])
     held = pltpu.VMEM((chunks, 4, rows, width), jnp.float32)
     sems = pltpu.SemaphoreType.DMA((chunks + 1,))
-    after, before, w_rows = call(
+    after, before, w_rows, early = call(
         lambda *refs: first_kernel(shape, chunks, devices, *refs),
         [
             (f32(chunks, 4, SUB * shape.steps, LANES), VMEM), (near, VMEM), (f32(chunks * SUB, LANES), VMEM),
+            (near, VMEM),
         ],
         [
             (fields_in, HBM), (flight_angular, HBM), (model, VMEM), (surface_angular, HBM), (records, HBM), (positions, HBM),
@@ -665,7 +685,6 @@
         (after, VMEM), (w_rows, VMEM), (mate, VMEM), (two, VMEM), (mate_two, VMEM),
     ]
     again = work_scratch(shape, 2)
-    both = f32(2 * LAYERS * parts, cells)
     sent1, next_a = call(
         lambda *refs: next_kernel(shape, freqs, devices, 0, *refs),
         [(f32(4 * rows, width), VMEM), (f32(2 * LAYERS * parts, cells), VMEM)],
@@ -674,45 +693,54 @@
         "next",
     )
     first = lax.ppermute(sent1, axis, via)
-    sent2, own, next1, next2, up, shared = call(
+    sent2, own, shared, across, next2 = call(
         lambda *refs: next_kernel(shape, freqs, devices, 1, *refs),
-        [(chunk, VMEM), (near, VMEM), (near, VMEM), (near, VMEM), (row, VMEM), (both, VMEM)],
+        [(chunk, VMEM)] + [(near, VMEM)] * 4,
         common + [(before, VMEM), (next_a, VMEM)],
         [image_scratch(2)] + again,
         "next",
     )
     second = lax.ppermute(sent2, axis, on)
     other = swapped(shared)
-    (mixed,) = call(mix_kernel, [(both, VMEM)], [(next1, VMEM), (next2, VMEM), (up, VMEM), (other, VMEM)], [], "mix")
     crossed = lax.ppermute(
-        mixed, axis, [(i, (i + 1) % devices) for i in range(1, devices, 2)] + [(i, i - 1) for i in range(2, devices, 2)]
-    )
-    relayed = lax.ppermute(lax.optimization_barrier((first, mixed))[0], axis, relay)
-    top1, late, extra = call(
+        across, axis, [(i, (i + 1) % devices) for i in range(1, devices, 2)] + [(i, i - 1) for i in range(2, devices, 2)]
+    )
+    from2 = lax.ppermute(next2, axis, [(i, i + 2) for i in range(devices - 2)] + [(last, 1)])
+    relayed = lax.ppermute(first, axis, relay)
+    half_shape = f32(4 * rows, width)
+    top1, more, late, extra = call(
         lambda *refs: late_kernel(shape, chunks, devices, *refs),
-        [(f32(4, freqs, width), ANY), (near, VMEM), (near, VMEM)],
+        [(half_shape, VMEM), (half_shape, VMEM), (near, VMEM), (near, VMEM)],
         [
             (fields_in, HBM), (flight_angular, HBM), (surface_angular, HBM), (wavelet, HBM), (source_pos, SMEM),
-            (planes1, ANY), (model, VMEM), (mate, VMEM), (mixed, VMEM),
+            (planes1, ANY), (model, VMEM), (mate, VMEM), (early, VMEM), (own, VMEM),
         ],
         [
-            held, planes_scratch, pltpu.VMEM((4, freqs, width), jnp.float32), image_scratch(1),
+            held, planes_scratch, image_scratch(1),
             row_of(flight_angular), row_of(surface_angular), row_of(wavelet), sems,
         ]
         + work_scratch(shape, 1),
         "late",
     )
-    (passing,) = call(pass_kernel, [(near, VMEM)], [(crossed, VMEM), (late, VMEM)], [], "pass")
-    passed = swapped(passing)
+    late = swapped(late)
+    more = lax.ppermute(more, axis, [(0, 1)])
+    (placed,) = call(
+        place_kernel,
+        [(f32(1, 4, freqs, width), ANY)],
+        [(first, VMEM), (relayed, VMEM), (top, ANY), (top1, VMEM), (more, VMEM)],
+        [pltpu.SemaphoreType.DMA((8,))],
+        "place",
+    )
     section, fields_out = call(
         close_kernel,
         [(f32(LAYERS, width), VMEM), (f32(1, 4, freqs, width), ANY)],
         [
-            (first, VMEM), (relayed, VMEM), (second, VMEM), (top, ANY), (top1, ANY),
-            (own, VMEM), (other, VMEM), (crossed, VMEM), (passed, VMEM), (extra, VMEM),
+            (placed, ANY), (second, VMEM), (own, VMEM), (other, VMEM), (crossed, VMEM), (from2, VMEM), (late, VMEM),
+            (extra, VMEM),
         ],
-        [pltpu.SemaphoreType.DMA((8,))],
+        [pltpu.SemaphoreType.DMA((4,))],
         "close",
+        {0: 1},
     )
     return section, fields_out
 

time: 45.8 us -> 44.9 us (0.980)
  the two profiles are of different devices: /device:TPU:9 before, /device:TPU:11 now
where the time goes in v3:
time: 44.9 us; the launch traced here: 44.5 us
  starting transfers between devices  19 us (42%)
  Pallas kernels  15.5 us (35%)
  waiting for transfers between devices  8.35 us (19%)
  between operations  1.6 us (4%)
    pallas_call x7, Pallas kernels, call(): pl.pallas_call(body, out_shape=[shape for shape, _ in outs], in_specs=[sp...  15.5 us
    ppermute x1, starting transfers between devices, on_device(): relayed = lax.ppermute(first, axis, relay)  4.32 us
    ppermute x1, waiting for transfers between devices, on_device(): relayed = lax.ppermute(first, axis, relay)  3.47 us
    ppermute x1, starting transfers between devices, on_device(): first = lax.ppermute(sent1, axis, via)  3.44 us
    ppermute x1, starting transfers between devices, on_device(): lax.ppermute(next2, axis, [(i, i + 2) for i in range(devices - 2)] + [(la...  3.44 us
    ppermute x1, waiting for transfers between devices, on_device(): lax.ppermute(next2, axis, [(i, i + 2) for i in range(devices - 2)] + [(la...  2.68 us
    ppermute x1, starting transfers between devices, on_device(): second = lax.ppermute(sent2, axis, on)  2.51 us
    ppermute x1, starting transfers between devices, on_device(): lax.ppermute(across, axis, [(i, (i + 1) % devices) for i in range(1, devi...  1.94 us
  transfers between devices with their start and end apart: 11, of which 5 were waited for; matrix products, arithmetic and copies ran while one was open for 0% of the time, Pallas kernels for 22%

profile of v3, /device:TPU:11, one launch (start us, length us, event | category | flops | bytes accessed | tf_op | source)
XLA Modules:
  0.0 44.5 jit_solution(13768544187210746807)
XLA Ops:
  1.3 0.8 %begin.1 = (f32[40,256]{1,0:T(8,128)S(1)}, f32[2,32,2048]{2,1,0:T(8,128)S(1)}, f32[4,32,2048]{2,1,0:T(8,128)S(1)}) custom-call(f32[4,16]{1,0:T(4,128)} %refs_0_.3, s32[4,2048]{1,0:T(4,128)} %refs_1_.3, f32[3,2,32,1024]{3,2,1,0:T(8,128)} %refs_4_.4, s32[1,1024]{1,0:T(1,128)} %bitcast.1, f32[3,2,32]{2,1,0:T(2,128)} %refs_3_.3, s32[1]{0:T(128)S(6)} %copy.13.refs_5_.refs_7_.refs_4_), custom_call_target="tpu_custom_call" | custom-call | tf_op jit(solution)/shard_map/begin/pallas_call | solution.py:631
  2.1 0.7 %collective-permute-start = (f32[40,256]{1,0:T(8,128)S(1)}, f32[40,256]{1,0:T(8,128)S(1)}, u32[]{:S(2)}, u32[]{:S(2)}) collective-permute-start(f32[40,256]{1,0:T(8,128)S(1)} %get-tuple-element.25.refs_2_.refs_6_), channel_id=1, source_target_pairs={{0,1},{1,0},{2,3},{3,2},{4,5},{5,4},{6,7},{7,6},{8,9},{9,8},{10,11... | collective-permute-start | bytes 122888 | tf_op jit(solution)/shard_map/ppermute | solution.py:644
  2.8 0.9 %collective-permute-done.refs_2_.refs_7_ = f32[40,256]{1,0:T(8,128)S(1)} collective-permute-done((f32[40,256]{1,0:T(8,128)S(1)}, f32[40,256]{1,0:T(8,128)S(1)}, u32[]{:S(2)}, u32[]{:S(2)}) %collective-permute-start) | collective-permute-done | bytes 40992 | tf_op jit(solution)/shard_map/ppermute | solution.py:644
  3.7 1.1 %collective-permute-start.1 = (f32[40,256]{1,0:T(8,128)S(1)}, f32[40,256]{1,0:T(8,128)S(1)}, u32[]{:S(2)}, u32[]{:S(2)}) collective-permute-start(f32[40,256]{1,0:T(8,128)S(1)} %get-tuple-element.25.refs_2_.refs_6_), channel_id=1, source_target_pairs={{0,14},{1,15},{2,0},{3,1},{4,2},{5,3},{6,4},{7,5},{8,6},{9,7},{10,... | collective-permute-start | bytes 122888 | tf_op jit(solution)/shard_map/ppermute | solution.py:664
  4.8 5.2 %first.1 = (f32[2,4,256,128]{3,2,1,0:T(8,128)S(1)}, f32[32,256]{1,0:T(8,128)S(1)}, f32[16,128]{1,0:T(8,128)S(1)}, f32[32,256]{1,0:T(8,128)S(1)}) custom-call(f32[1,4,32,2048]{3,2,1,0:T(8,128)} %refs_0_.5, f32[1,32]{1,0:T(1,128)} %refs_1_.5, f32[40,256]{1,0:T(8,128)S(1)} %get-tuple-element.25.refs_2_.refs_6_, f32[3,32]{1,0:T(4,128)} %refs_2_.3, ...), custom_call_target="tpu_custom_call" | custom-call | tf_op jit(solution)/shard_map/first/pallas_call | solution.py:631
  10.0 0.0 collective-permute-done.1.refs_3_
  10.0 0.7 %collective-permute-start.2 = (f32[40,256]{1,0:T(8,128)S(1)}, f32[40,256]{1,0:T(8,128)S(1)}, u32[]{:S(2)}, u32[]{:S(2)}) collective-permute-start(f32[40,256]{1,0:T(8,128)S(1)} %collective-permute-done.1.refs_3_), channel_id=1, source_target_pairs={{0,1},{1,0},{2,3},{3,2},{4,5},{5,4},{6,7},{7,6},{8,9},{9,8},{10,11... | collective-permute-start | bytes 122888 | tf_op jit(solution)/shard_map/ppermute | solution.py:644
  10.7 0.9 %collective-permute-done.2.refs_4_ = f32[40,256]{1,0:T(8,128)S(1)} collective-permute-done((f32[40,256]{1,0:T(8,128)S(1)}, f32[40,256]{1,0:T(8,128)S(1)}, u32[]{:S(2)}, u32[]{:S(2)}) %collective-permute-start.2) | collective-permute-done | bytes 40992 | tf_op jit(solution)/shard_map/ppermute | solution.py:644
  11.6 3.6 %next.2 = (f32[64,2048]{1,0:T(8,128)S(1)}, f32[64,256]{1,0:T(8,128)S(1)}) custom-call(f32[2,4,256,128]{3,2,1,0:T(8,128)S(1)} %get-tuple-element.23.refs_0_, f32[16,128]{1,0:T(8,128)S(1)} %get-tuple-element.24.refs_1_, f32[40,256]{1,0:T(8,128)S(1)} %collective-permute-done.refs_2_.refs_7_, f32[40,256]{1,0:T(8,128)S(1)} %collective-permute-done.1.refs_3_, ...), custom_call_target="tpu_custom_call" | custom-call | tf_op jit(solution)/shard_map/next/pallas_call | solution.py:631
  15.2 3.4 %collective-permute-start.3 = (f32[64,2048]{1,0:T(8,128)S(1)}, f32[64,2048]{1,0:T(8,128)S(1)}, u32[]{:S(2)}, u32[]{:S(2)}) collective-permute-start(f32[64,2048]{1,0:T(8,128)S(1)} %get-tuple-element.27), channel_id=1, source_target_pairs={{0,3},{1,4},{2,1},{3,6},{4,7},{5,8},{6,5},{7,10},{8,11},{9,12},{10... | collective-permute-start | bytes 1572872 | tf_op jit(solution)/shard_map/ppermute | solution.py:695
  18.6 3.6 %next.3 = (f32[72,2048]{1,0:T(8,128)S(1)}, f32[32,256]{1,0:T(8,128)S(1)}, f32[32,256]{1,0:T(8,128)S(1)}, f32[32,256]{1,0:T(8,128)S(1)}, f32[32,256]{1,0:T(8,128)S(1)}) custom-call(f32[2,4,256,128]{3,2,1,0:T(8,128)S(1)} %get-tuple-element.23.refs_0_, f32[16,128]{1,0:T(8,128)S(1)} %get-tuple-element.24.refs_1_, ...), custom_call_target="tpu_custom_call" | custom-call | tf_op jit(solution)/shard_map/next/pallas_call | solution.py:631
  22.3 2.5 %collective-permute-start.6 = (f32[72,2048]{1,0:T(8,128)S(1)}, f32[72,2048]{1,0:T(8,128)S(1)}, u32[]{:S(2)}, u32[]{:S(2)}) collective-permute-start(f32[72,2048]{1,0:T(8,128)S(1)} %get-tuple-element.36), channel_id=1, source_target_pairs={{0,3},{1,4},{2,5},{3,6},{4,7},{5,8},{6,9},{7,10},{8,11},{9,12},{10... | collective-permute-start | bytes 1769480 | tf_op jit(solution)/shard_map/ppermute | solution.py:703
  24.8 0.7 %collective-permute-start.5 = (f32[64,2048]{1,0:T(8,128)S(1)}, f32[64,2048]{1,0:T(8,128)S(1)}, u32[]{:S(2)}, u32[]{:S(2)}) collective-permute-start(f32[64,2048]{1,0:T(8,128)S(1)} %get-tuple-element.35), channel_id=1, source_target_pairs={{0,1},{16,17}} | collective-permute-start | bytes 1572872 | tf_op jit(solution)/shard_map/ppermute | solution.py:726
  25.5 0.4 collective-permute-done.3.first
  26.0 4.3 %collective-permute-start.4 = (f32[64,2048]{1,0:T(8,128)S(1)}, f32[64,2048]{1,0:T(8,128)S(1)}, u32[]{:S(2)}, u32[]{:S(2)}) collective-permute-start(f32[64,2048]{1,0:T(8,128)S(1)} %collective-permute-done.3.first), channel_id=1, source_target_pairs={{1,5},{5,9},{9,13},{17,21},{21,25},{25,29}} | collective-permute-start | bytes 1572872 | tf_op jit(solution)/shard_map/ppermute | solution.py:709
  30.3 0.1 collective-permute-start.7
  30.4 1.9 %collective-permute-start.8 = (f32[32,256]{1,0:T(8,128)S(1)}, f32[32,256]{1,0:T(8,128)S(1)}, u32[]{:S(2)}, u32[]{:S(2)}) collective-permute-start(f32[32,256]{1,0:T(8,128)S(1)} %get-tuple-element.38), channel_id=1, source_target_pairs={{1,2},{3,4},{5,6},{7,8},{9,10},{11,12},{13,14},{15,0},{2,1},{4,3},... | collective-permute-start | bytes 98312 | tf_op jit(solution)/shard_map/ppermute | solution.py:705
  32.3 0.0 collective-permute-done.5.more
  32.3 3.4 %collective-permute-start.9 = (f32[32,256]{1,0:T(8,128)S(1)}, f32[32,256]{1,0:T(8,128)S(1)}, u32[]{:S(2)}, u32[]{:S(2)}) collective-permute-start(f32[32,256]{1,0:T(8,128)S(1)} %get-tuple-element.39), channel_id=1, source_target_pairs={{0,2},{1,3},{2,4},{3,5},{4,6},{5,7},{6,8},{7,9},{8,10},{9,11},{10,... | collective-permute-start | bytes 98312 | tf_op jit(solution)/shard_map/ppermute | solution.py:708
  35.8 3.5 %collective-permute-done.4.relayed = f32[64,2048]{1,0:T(8,128)S(1)} collective-permute-done((f32[64,2048]{1,0:T(8,128)S(1)}, f32[64,2048]{1,0:T(8,128)S(1)}, u32[]{:S(2)}, u32[]{:S(2)}) %collective-permute-start.4) | collective-permute-done | bytes 524320 | tf_op jit(solution)/shard_map/ppermute | solution.py:709
  39.3 0.0 collective-permute-start.10
  39.3 0.9 %place.1.placed = f32[1,4,32,2048]{3,2,1,0:T(8,128)} custom-call(f32[64,2048]{1,0:T(8,128)S(1)} %collective-permute-done.3.first, f32[64,2048]{1,0:T(8,128)S(1)} %collective-permute-done.4.relayed, f32[4,32,2048]{2,1,0:T(8,128)S(1)} %get-tuple-element.28.top, f32[64,2048]{1,0:T(8,128)S(1)} %get-tuple-element.34.top1, f32[64,2048]{1,0:T(8,128)S(1)} %collective-permute-done.5.more), custom_call_target="tpu_custom_call" | custom-call | tf_op jit(solution)/shard_map/place/pallas_call | solution.py:631
  40.1 0.0 collective-permute-done.7.other
  40.1 0.0 collective-permute-done.8.crossed
  40.2 2.7 %collective-permute-done.9.from2 = f32[32,256]{1,0:T(8,128)S(1)} collective-permute-done((f32[32,256]{1,0:T(8,128)S(1)}, f32[32,256]{1,0:T(8,128)S(1)}, u32[]{:S(2)}, u32[]{:S(2)}) %collective-permute-start.9) | collective-permute-done | bytes 32800 | tf_op jit(solution)/shard_map/ppermute | solution.py:708
  42.8 0.0 collective-permute-done.10.late
  42.8 0.0 collective-permute-done.6.second
  42.8 1.4 %close.1 = (f32[4,2048]{1,0:T(4,128)}, f32[1,4,32,2048]{3,2,1,0:T(8,128)}) custom-call(f32[1,4,32,2048]{3,2,1,0:T(8,128)} %place.1.placed, f32[72,2048]{1,0:T(8,128)S(1)} %collective-permute-done.6.second, f32[32,256]{1,0:T(8,128)S(1)} %get-tuple-element.33.refs_9_.own, f32[32,256]{1,0:T(8,128)S(1)} %collective-permute-done.7.other, ...), custom_call_target="tpu_custom_call", output_to_operand_aliasing={{1}: (0, {})} | custom-call | tf_op jit(solution)/shard_map/close/pallas_call | solution.py:631
  (1 shorter events, 0.0 us)
Async XLA Ops:
  2.1 1.6 %collective-permute-start = (f32[40,256]{1,0:T(8,128)S(1)}, f32[40,256]{1,0:T(8,128)S(1)}, u32[]{:S(2)}, u32[]{:S(2)}) collective-permute-start(f32[40,256]{1,0:T(8,128)S(1)} %get-tuple-element.25.refs_2_.refs_6_), channel_id=1, source_target_pairs={{0,1},{1,0},{2,3},{3,2},{4,5},{5,4},{6,7},{7,6},{8,9},{9,8},{10,11... | collective-permute-start | bytes 122888 | tf_op jit(solution)/shard_map/ppermute | solution.py:644
  3.7 6.3 %collective-permute-start.1 = (f32[40,256]{1,0:T(8,128)S(1)}, f32[40,256]{1,0:T(8,128)S(1)}, u32[]{:S(2)}, u32[]{:S(2)}) collective-permute-start(f32[40,256]{1,0:T(8,128)S(1)} %get-tuple-element.25.refs_2_.refs_6_), channel_id=1, source_target_pairs={{0,14},{1,15},{2,0},{3,1},{4,2},{5,3},{6,4},{7,5},{8,6},{9,7},{10,... | collective-permute-start | bytes 122888 | tf_op jit(solution)/shard_map/ppermute | solution.py:664
  10.0 1.6 %collective-permute-start.2 = (f32[40,256]{1,0:T(8,128)S(1)}, f32[40,256]{1,0:T(8,128)S(1)}, u32[]{:S(2)}, u32[]{:S(2)}) collective-permute-start(f32[40,256]{1,0:T(8,128)S(1)} %collective-permute-done.1.refs_3_), channel_id=1, source_target_pairs={{0,1},{1,0},{2,3},{3,2},{4,5},{5,4},{6,7},{7,6},{8,9},{9,8},{10,11... | collective-permute-start | bytes 122888 | tf_op jit(solution)/shard_map/ppermute | solution.py:644
  15.2 10.8 %collective-permute-start.3 = (f32[64,2048]{1,0:T(8,128)S(1)}, f32[64,2048]{1,0:T(8,128)S(1)}, u32[]{:S(2)}, u32[]{:S(2)}) collective-permute-start(f32[64,2048]{1,0:T(8,128)S(1)} %get-tuple-element.27), channel_id=1, source_target_pairs={{0,3},{1,4},{2,1},{3,6},{4,7},{5,8},{6,5},{7,10},{8,11},{9,12},{10... | collective-permute-start | bytes 1572872 | tf_op jit(solution)/shard_map/ppermute | solution.py:695
  22.3 20.6 %collective-permute-start.6 = (f32[72,2048]{1,0:T(8,128)S(1)}, f32[72,2048]{1,0:T(8,128)S(1)}, u32[]{:S(2)}, u32[]{:S(2)}) collective-permute-start(f32[72,2048]{1,0:T(8,128)S(1)} %get-tuple-element.36), channel_id=1, source_target_pairs={{0,3},{1,4},{2,5},{3,6},{4,7},{5,8},{6,9},{7,10},{8,11},{9,12},{10... | collective-permute-start | bytes 1769480 | tf_op jit(solution)/shard_map/ppermute | solution.py:703
  24.8 7.5 %collective-permute-start.5 = (f32[64,2048]{1,0:T(8,128)S(1)}, f32[64,2048]{1,0:T(8,128)S(1)}, u32[]{:S(2)}, u32[]{:S(2)}) collective-permute-start(f32[64,2048]{1,0:T(8,128)S(1)} %get-tuple-element.35), channel_id=1, source_target_pairs={{0,1},{16,17}} | collective-permute-start | bytes 1572872 | tf_op jit(solution)/shard_map/ppermute | solution.py:726
  26.0 13.3 %collective-permute-start.4 = (f32[64,2048]{1,0:T(8,128)S(1)}, f32[64,2048]{1,0:T(8,128)S(1)}, u32[]{:S(2)}, u32[]{:S(2)}) collective-permute-start(f32[64,2048]{1,0:T(8,128)S(1)} %collective-permute-done.3.first), channel_id=1, source_target_pairs={{1,5},{5,9},{9,13},{17,21},{21,25},{25,29}} | collective-permute-start | bytes 1572872 | tf_op jit(solution)/shard_map/ppermute | solution.py:709
  30.3 9.8 %collective-permute-start.7 = (f32[32,256]{1,0:T(8,128)S(1)}, f32[32,256]{1,0:T(8,128)S(1)}, u32[]{:S(2)}, u32[]{:S(2)}) collective-permute-start(f32[32,256]{1,0:T(8,128)S(1)} %get-tuple-element.37), channel_id=1, source_target_pairs={{0,1},{1,0},{2,3},{3,2},{4,5},{5,4},{6,7},{7,6},{8,9},{9,8},{10,11... | collective-permute-start | bytes 98312 | tf_op jit(solution)/shard_map/ppermute | solution.py:644
  30.4 9.8 %collective-permute-start.8 = (f32[32,256]{1,0:T(8,128)S(1)}, f32[32,256]{1,0:T(8,128)S(1)}, u32[]{:S(2)}, u32[]{:S(2)}) collective-permute-start(f32[32,256]{1,0:T(8,128)S(1)} %get-tuple-element.38), channel_id=1, source_target_pairs={{1,2},{3,4},{5,6},{7,8},{9,10},{11,12},{13,14},{15,0},{2,1},{4,3},... | collective-permute-start | bytes 98312 | tf_op jit(solution)/shard_map/ppermute | solution.py:705
  32.3 10.5 %collective-permute-start.9 = (f32[32,256]{1,0:T(8,128)S(1)}, f32[32,256]{1,0:T(8,128)S(1)}, u32[]{:S(2)}, u32[]{:S(2)}) collective-permute-start(f32[32,256]{1,0:T(8,128)S(1)} %get-tuple-element.39), channel_id=1, source_target_pairs={{0,2},{1,3},{2,4},{3,5},{4,6},{5,7},{6,8},{7,9},{8,10},{9,11},{10,... | collective-permute-start | bytes 98312 | tf_op jit(solution)/shard_map/ppermute | solution.py:708
  39.3 3.6 %collective-permute-start.10 = (f32[32,256]{1,0:T(8,128)S(1)}, f32[32,256]{1,0:T(8,128)S(1)}, u32[]{:S(2)}, u32[]{:S(2)}) collective-permute-start(f32[32,256]{1,0:T(8,128)S(1)} %get-tuple-element.40), channel_id=1, source_target_pairs={{0,1},{1,0},{2,3},{3,2},{4,5},{5,4},{6,7},{7,6},{8,9},{9,8},{10,11... | collective-permute-start | bytes 98312 | tf_op jit(solution)/shard_map/ppermute | solution.py:644
